TPU v7x, 256 devices: a whole 4x4x8 slice. The times are simulated.
256 devices in a mesh: seq: 64 (over y_lo, z, x), head: 4 (over y_hi, core).
Axes of the slice: x: 4, y: 4 (y_hi: 2, y_lo: 2; y = y_hi * 2 + y_lo), z: 8, core: 2. Of those that a mesh axis runs over, the one named last changes fastest.
Arguments:
- queries: bfloat16 [65536, 4096], P('seq', 'head'), may hold values from -120 to 120
- keys: bfloat16 [65536, 512], P('seq', 'head'), may hold values from -6 to 6
- values: bfloat16 [65536, 512], P('seq', 'head'), may hold values from -6 to 6
- mid_pool: bfloat16 [4, 8], P('head'), may hold values from -3 to 3
- coarse_pool: bfloat16 [4, 256], P('head'), may hold values from -0.375 to 0.375
Outputs:
- attended: bfloat16 [65536, 4096], P(('seq', 'head'))
All inputs are finite; a program needn't handle non-finite values.
Results may differ from a plain program's by a relative error of at most 0.0092.
Values may be sent and summed in bfloat16 or wider, within the bound.
A program may use at most 128 MiB of HBM per device.

v0:
```python
import math

import jax
import jax.numpy as jnp
from jax import lax
from jax.sharding import PartitionSpec as P

HEAD_DIM = 128
BLK = 256
GROUP = 8
MIDS = 256
MIDB = 8


def passed_along(array, axis, by):
    size = lax.axis_size(axis)
    pairs = [(i, i + by) for i in range(size) if 0 <= i + by < size]
    return lax.ppermute(array, axis, pairs)


def in_one_piece(arrays, axis, dim, along):
    both = jnp.concatenate(arrays, axis=along)
    whole, at, outs = (lax.all_gather(both, axis, axis=dim, tiled=True), 0, [])
    for a in arrays:
        outs.append(lax.slice_in_dim(whole, at, at + a.shape[along], axis=along))
        at += a.shape[along]
    return tuple(outs)


def summarize(source, pooling, group_size, kv_here):
    rows_here = source.shape[0]
    grouped = source.reshape(rows_here // group_size, group_size, kv_here, HEAD_DIM)
    summary = jnp.einsum("gthd,ht->ghd", grouped, pooling, preferred_element_type=jnp.float32)
    return summary.astype(jnp.bfloat16).reshape(rows_here // group_size, kv_here * HEAD_DIM)


def body(queries, keys, values, mid_pool, coarse_pool):
    tokens_here = queries.shape[0]
    columns = queries.shape[1]
    kv_columns = keys.shape[1]
    kv_here = kv_columns // HEAD_DIM
    sharing = columns // HEAD_DIM // kv_here
    block_count = tokens_here // BLK
    per_group = BLK // GROUP
    hop_count = (MIDB + block_count) // block_count
    device = lax.axis_index("seq")
    logit_scale = 1.0 / math.sqrt(HEAD_DIM)
    mid_keys = summarize(keys, mid_pool, GROUP, kv_here)
    mid_values = summarize(values, mid_pool, GROUP, kv_here)
    summary_key_rows = summarize(keys, coarse_pool, BLK, kv_here)
    coarse_values = summarize(values, coarse_pool, BLK, kv_here)
    tail_keys, tail_values, near_mid_k, near_mid_v = passed_along(
        (keys[tokens_here - BLK :], values[tokens_here - BLK :], mid_keys, mid_values), "seq", 1
    )
    arrivals = [(near_mid_k, near_mid_v)]
    carried = (near_mid_k, near_mid_v)
    for distance in range(2, hop_count + 1):
        carried = passed_along((carried[0], carried[1]), "seq", 1)
        arrivals.append(carried)
    mid_shape = ((hop_count + 1) * block_count, per_group, kv_here, HEAD_DIM)
    mid_blocks_k = jnp.concatenate([pair[0] for pair in arrivals[::-1]] + [mid_keys]).reshape(
        mid_shape
    )
    mid_blocks_v = jnp.concatenate([pair[1] for pair in arrivals[::-1]] + [mid_values]).reshape(
        mid_shape
    )
    all_coarse_k, all_coarse_v = in_one_piece((summary_key_rows, coarse_values), "seq", 0, 1)
    coarse_total = all_coarse_k.shape[0]
    all_coarse_k = all_coarse_k.reshape(coarse_total, kv_here, HEAD_DIM)
    all_coarse_v = all_coarse_v.reshape(coarse_total, kv_here, HEAD_DIM)
    block_shape = (block_count + 1, BLK, kv_here, HEAD_DIM)
    key_blocks = jnp.concatenate([tail_keys, keys]).reshape(block_shape)
    value_blocks = jnp.concatenate([tail_values, values]).reshape(block_shape)
    blocked_queries = queries.reshape(block_count, BLK, kv_here, sharing, HEAD_DIM)
    step_blocks = min(block_count, max(1, 512 // BLK))
    pieces = []
    for start_block in range(0, block_count, step_blocks):
        stop_block = start_block + step_blocks
        query_rows = blocked_queries[start_block:stop_block]
        local_keys = jnp.concatenate(
            [key_blocks[start_block:stop_block], key_blocks[start_block + 1 : stop_block + 1]],
            axis=1,
        )
        near_values = jnp.concatenate(
            [value_blocks[start_block:stop_block], value_blocks[start_block + 1 : stop_block + 1]],
            axis=1,
        )
        mid_start = hop_count * block_count - 1 - MIDB + start_block
        far_keys = jnp.concatenate(
            [
                mid_blocks_k[mid_start + offset : mid_start + offset + step_blocks]
                for offset in range(MIDB)
            ],
            axis=1,
        )
        far_values = jnp.concatenate(
            [
                mid_blocks_v[mid_start + offset : mid_start + offset + step_blocks]
                for offset in range(MIDB)
            ],
            axis=1,
        )
        local_scores = (
            jnp.einsum(
                "bqhsd,bkhd->bhsqk", query_rows, local_keys, preferred_element_type=jnp.float32
            )
            * logit_scale
        )
        middle_level_scores = (
            jnp.einsum(
                "bqhsd,bkhd->bhsqk", query_rows, far_keys, preferred_element_type=jnp.float32
            )
            * logit_scale
        )
        summary_score_rows = (
            jnp.einsum(
                "bqhsd,chd->bhsqc", query_rows, all_coarse_k, preferred_element_type=jnp.float32
            )
            * logit_scale
        )
        block_ids = (device * block_count + start_block + jnp.arange(step_blocks, dtype=jnp.int32))[
            :, None, None, None, None
        ]
        query_pos = block_ids * BLK + jnp.arange(BLK, dtype=jnp.int32)[None, None, None, :, None]
        key_pos = (
            block_ids * BLK - BLK + jnp.arange(2 * BLK, dtype=jnp.int32)[None, None, None, None, :]
        )
        near_ok = (key_pos >= 0) & (key_pos <= query_pos)
        mid_ok = (block_ids - 1 - MIDB) * per_group + jnp.arange(MIDS, dtype=jnp.int32)[
            None, None, None, None, :
        ] >= 0
        coarse_ok = (
            jnp.arange(coarse_total, dtype=jnp.int32)[None, None, None, None, :]
            <= block_ids - MIDB - 2
        )
        scores = jnp.concatenate(
            [
                jnp.where(near_ok, local_scores, -jnp.inf),
                jnp.where(mid_ok, middle_level_scores, -jnp.inf),
                jnp.where(coarse_ok, summary_score_rows, -jnp.inf),
            ],
            axis=-1,
        )
        row_max = jnp.max(scores, axis=-1, keepdims=True)
        exponent = jnp.exp(scores - row_max)
        row_total = jnp.sum(exponent, axis=-1, keepdims=True)
        softmax_weights = (exponent / row_total).astype(jnp.bfloat16)
        near_part = softmax_weights[..., : 2 * BLK]
        mid_part = softmax_weights[..., 2 * BLK : 2 * BLK + MIDS]
        coarse_part = softmax_weights[..., 2 * BLK + MIDS :]
        output_rows = jnp.einsum(
            "bhsqk,bkhd->bqhsd", near_part, near_values, preferred_element_type=jnp.float32
        )
        output_rows = output_rows + jnp.einsum(
            "bhsqk,bkhd->bqhsd", mid_part, far_values, preferred_element_type=jnp.float32
        )
        output_rows = output_rows + jnp.einsum(
            "bhsqc,chd->bqhsd", coarse_part, all_coarse_v, preferred_element_type=jnp.float32
        )
        pieces.append(output_rows.astype(jnp.bfloat16).reshape(step_blocks * BLK, columns))
    attended = jnp.concatenate(pieces, axis=0)
    return lax.all_to_all(attended, "head", split_axis=0, concat_axis=1, tiled=True)


def solution(mesh):
    return jax.shard_map(
        body,
        mesh=mesh,
        in_specs=(
            P("seq", "head"),
            P("seq", "head"),
            P("seq", "head"),
            P("head", None),
            P("head", None),
        ),
        out_specs=P(("seq", "head"), None),
        check_vma=False,
    )
```

profile of v0, /device:TPU:224, one launch (start us, length us, event | category | flops | bytes accessed | tf_op | source)
XLA Modules:
  0.0 296.3 jit_solution(15995833833225870521)
XLA Ops:
  0.0 1.2 fusion.30
  1.3 3.4 %collective-permute-start.2 = (bf16[128,128]{1,0:T(8,128)(2,1)S(1)}, bf16[128,128]{1,0:T(8,128)(2,1)S(1)}, u32[]{:S(2)}, u32[]{:S(2)}) collective-permute-start(bf16[128,128]{1,0:T(8,128)(2,1)S(1)} %convert_element_type.44), channel_id=1, source_target_pairs={{0,4},{4,8},{8,12},{12,16},{16,20},{20,24},{24,28},{28,32},{32,36}... | collective-permute-start | bytes 98312 | tf_op jit(solution)/shard_map/ppermute | solution.py:18
  4.7 1.5 slice.249
  6.1 3.4 %collective-permute-start.1 = (bf16[256,128]{1,0:T(8,128)(2,1)}, bf16[256,128]{1,0:T(8,128)(2,1)}, u32[]{:S(2)}, u32[]{:S(2)}) collective-permute-start(bf16[256,128]{1,0:T(8,128)(2,1)} %slice.249), channel_id=1, source_target_pairs={{0,4},{4,8},{8,12},{12,16},{16,20},{20,24},{24,28},{28,32},{32,36}... | collective-permute-start | bytes 196616 | tf_op jit(solution)/shard_map/ppermute | solution.py:18
  9.5 1.2 fusion.28
  10.7 3.1 %collective-permute-start.5 = (bf16[128,128]{1,0:T(8,128)(2,1)S(1)}, bf16[128,128]{1,0:T(8,128)(2,1)S(1)}, u32[]{:S(2)}, u32[]{:S(2)}) collective-permute-start(bf16[128,128]{1,0:T(8,128)(2,1)S(1)} %convert_element_type.48), channel_id=1, source_target_pairs={{0,4},{4,8},{8,12},{12,16},{16,20},{20,24},{24,28},{28,32},{32,36}... | collective-permute-start | bytes 98312 | tf_op jit(solution)/shard_map/ppermute | solution.py:18
  13.8 1.5 slice.244
  15.3 1.9 collective-permute-start
  17.6 2.7 slice_bitcast_fusion.17
  20.3 0.3 copy.147
  20.7 0.1 fusion.38
  20.8 0.2 fusion.36
  21.0 144.6 %all-gather = bf16[64,4,256]{2,1,0:T(4,128)(2,1)S(1)} all-gather(bf16[1,4,256]{2,1,0:T(4,128)(2,1)S(1)} %maximum_bitcast_fusion.8), channel_id=1, replica_groups=mesh['seq'=64,'head'=4] {'seq'}, dimensions={0}, use_global_device_ids=true | all-gather | bytes 133120 | tf_op jit(solution)/shard_map/all_gather | solution.py:23
  165.7 1.5 copy.149
  167.3 2.8 fusion.55
  170.1 3.3 %fusion.52 = (f32[2,8,256]{2,1,0:T(8,128)}, f32[2,1,8,256,256]{3,4,2,0,1:T(8,128)}) fusion(bf16[2,256,8,128]{3,2,1,0:T(8,128)(2,1)S(1)} %bitcast.240, bf16[256,256]{1,0:T(8,128)(2,1)S(1)} %reshape.711, pred[2,256]{1,0:T(4,128)(4,1)S(1)} %iota_compare_fusion), kind=kOutput, calls=%fused_computation.126 | convolution fusion | flops 271577088 | bytes 5325824 | tf_op jit(solution)/shard_map/bqhsd,chd->bhsqc/dot_general | solution.py:116
  173.4 0.3 compare_and_fusion.1
  173.7 0.3 compare_and_fusion
  174.2 3.8 %collective-permute-start.3 = (bf16[128,128]{1,0:T(8,128)(2,1)S(1)}, bf16[128,128]{1,0:T(8,128)(2,1)S(1)}, u32[]{:S(2)}, u32[]{:S(2)}) collective-permute-start(bf16[128,128]{1,0:T(8,128)(2,1)S(1)} %collective-permute-done.2), channel_id=1, source_target_pairs={{0,4},{4,8},{8,12},{12,16},{16,20},{20,24},{24,28},{28,32},{32,36}... | collective-permute-start | bytes 98312 | tf_op jit(solution)/shard_map/ppermute | solution.py:18
  177.9 4.2 %collective-permute-start.6 = (bf16[128,128]{1,0:T(8,128)(2,1)S(1)}, bf16[128,128]{1,0:T(8,128)(2,1)S(1)}, u32[]{:S(2)}, u32[]{:S(2)}) collective-permute-start(bf16[128,128]{1,0:T(8,128)(2,1)S(1)} %collective-permute-done.5), channel_id=1, source_target_pairs={{0,4},{4,8},{8,12},{12,16},{16,20},{20,24},{24,28},{28,32},{32,36}... | collective-permute-start | bytes 98312 | tf_op jit(solution)/shard_map/ppermute | solution.py:18
  182.1 0.9 pad_maximum_fusion.1
  183.0 4.6 %fusion.56 = (f32[2,8,256]{2,1,0:T(8,128)S(1)}, f32[2,1,8,256,512]{3,4,2,0,1:T(8,128)}) fusion(bf16[2,256,8,128]{3,2,1,0:T(8,128)(2,1)S(1)} %bitcast.244, bf16[2,256,1,128]{3,1,0,2:T(8,128)(2,1)S(1)} %bitcast.258, bf16[2,256,1,128]{3,1,0,2:T(8,128)(2,1)S(1)} %bitcast.257, pred[2,256,512]{1,2,0:T(8,128)(4,1)S(1)} %compare_and_fusion.1), kind=kOutput, calls=%fused_computation.130 | convolution fusion | flops 543682560 | bytes 9977856 | tf_op jit(solution)/shard_map/bqhsd,bkhd->bhsqk/dot_general | solution.py:104
  187.6 5.3 %fusion.53 = (f32[2,8,256]{2,1,0:T(8,128)}, f32[2,1,8,256,512]{3,4,2,0,1:T(8,128)}) fusion(bf16[2,256,8,128]{3,2,1,0:T(8,128)(2,1)S(1)} %bitcast.241, bf16[2,256,1,128]{3,1,0,2:T(8,128)(2,1)S(1)} %bitcast.255, bf16[2,256,1,128]{3,1,0,2:T(8,128)(2,1)S(1)} %bitcast.256, pred[2,256,512]{1,2,0:T(8,128)(4,1)S(1)} %compare_and_fusion), kind=kOutput, calls=%fused_computation.127 | convolution fusion | flops 543682560 | bytes 9977856 | tf_op jit(solution)/shard_map/bqhsd,bkhd->bhsqk/dot_general | solution.py:104
  192.9 5.9 %collective-permute-start.4 = (bf16[128,128]{1,0:T(8,128)(2,1)S(1)}, bf16[128,128]{1,0:T(8,128)(2,1)S(1)}, u32[]{:S(2)}, u32[]{:S(2)}) collective-permute-start(bf16[128,128]{1,0:T(8,128)(2,1)S(1)} %collective-permute-done.3), channel_id=1, source_target_pairs={{0,4},{4,8},{8,12},{12,16},{16,20},{20,24},{24,28},{28,32},{32,36}... | collective-permute-start | bytes 98312 | tf_op jit(solution)/shard_map/ppermute | solution.py:18
  198.8 0.9 pad_maximum_fusion.2
  199.9 0.8 copy.106
  200.7 0.8 copy.107
  201.5 8.8 %collective-permute-start.7 = (bf16[128,128]{1,0:T(8,128)(2,1)S(1)}, bf16[128,128]{1,0:T(8,128)(2,1)S(1)}, u32[]{:S(2)}, u32[]{:S(2)}) collective-permute-start(bf16[128,128]{1,0:T(8,128)(2,1)S(1)} %collective-permute-done.6), channel_id=1, source_target_pairs={{0,4},{4,8},{8,12},{12,16},{16,20},{20,24},{24,28},{28,32},{32,36}... | collective-permute-start | bytes 98312 | tf_op jit(solution)/shard_map/ppermute | solution.py:18
  210.3 0.6 fusion.51
  211.1 1.0 fusion.57
  212.1 5.7 %fusion.3 = f32[2,8,256]{2,1,0:T(8,128)S(1)} fusion(f32[2,1,8,256,256]{3,4,2,0,1:T(8,128)S(1)} %copy-done.3, f32[2,1,8,256,256]{3,4,2,0,1:T(8,128)S(1)} %get-tuple-element.58, f32[2,1,8,256,512]{3,4,2,0,1:T(8,128)} %get-tuple-element.56, f32[2,8,256]{2,1,0:T(8,128)S(1)} %maximum_maximum_fusion.1), kind=kLoop, calls=%fused_computation.7 | loop fusion | flops 16773120 | bytes 16809984 | tf_op jit(solution)/shard_map/reduce_sum | solution.py:146
  217.9 4.9 %divide_convert_fusion.1 = bf16[2,1,8,256,1024]{3,4,2,0,1:T(8,128)(2,1)} fusion(f32[2,1,8,256,256]{3,4,2,0,1:T(8,128)S(1)} %copy-done.3, f32[2,1,8,256,256]{3,4,2,0,1:T(8,128)S(1)} %get-tuple-element.58, f32[2,1,8,256,512]{3,4,2,0,1:T(8,128)S(1)} %bitcast.239, f32[2,8,256]{2,1,0:T(8,128)S(1)} %fusion.3, f32[2,8,256]{2,1,0:T(8,128)S(1)} %maximum_maximum_fusion.1), kind=kLoop, calls=%fused_computation.5 | loop fusion | flops 20971520 | bytes 25198592 | tf_op jit(solution)/shard_map/convert_element_type | solution.py:147
  222.7 0.6 fusion.50
  223.4 0.1 copy.100
  223.5 0.1 copy.101
  223.6 0.1 copy.96
  223.8 0.1 copy.97
  223.9 0.1 copy.98
  224.0 0.1 copy.99
  224.2 0.1 copy.94
  224.3 0.1 copy.95
  224.4 0.2 concatenate.97
  224.6 2.1 fusion.11
  226.7 2.9 fusion.5
  229.6 2.3 fusion.13
  231.9 0.7 copy.105
  232.7 1.2 copy.178
  233.9 1.7 constant_dynamic-update-slice_fusion.9
  235.6 1.3 constant_dynamic-update-slice_fusion.8
  237.0 1.8 fusion.54
  238.8 5.4 %fusion.2 = f32[2,8,256]{2,1,0:T(8,128)S(1)} fusion(f32[2,1,8,256,256]{3,4,2,0,1:T(8,128)S(1)} %copy-done.2, f32[2,1,8,256,256]{3,4,2,0,1:T(8,128)S(1)} %get-tuple-element.52, f32[2,1,8,256,512]{3,4,2,0,1:T(8,128)} %get-tuple-element.50, f32[2,8,256]{2,1,0:T(8,128)S(1)} %maximum_maximum_fusion), kind=kLoop, calls=%fused_computation.6 | loop fusion | flops 16773120 | bytes 16809984 | tf_op jit(solution)/shard_map/reduce_sum | solution.py:146
  244.3 5.0 %divide_convert_fusion = bf16[2,1,8,256,1024]{3,4,2,0,1:T(8,128)(2,1)} fusion(f32[2,1,8,256,256]{3,4,2,0,1:T(8,128)S(1)} %copy-done.2, f32[2,1,8,256,256]{3,4,2,0,1:T(8,128)S(1)} %get-tuple-element.52, f32[2,1,8,256,512]{3,4,2,0,1:T(8,128)S(1)} %bitcast.237, f32[2,8,256]{2,1,0:T(8,128)S(1)} %fusion.2, f32[2,8,256]{2,1,0:T(8,128)S(1)} %maximum_maximum_fusion), kind=kLoop, calls=%fused_computation.4 | loop fusion | flops 20971520 | bytes 25198592 | tf_op jit(solution)/shard_map/convert_element_type | solution.py:147
  249.3 0.1 copy.118
  249.4 0.1 copy.119
  249.6 0.2 concatenate.104
  249.8 2.1 fusion.9
  251.9 2.9 fusion.4
  254.8 2.4 fusion.12
  257.2 0.7 copy.123
  257.9 0.3 copy.177
  258.2 0.3 pad_maximum_fusion
  258.5 31.2 %all_to_all.19 = bf16[4,256,1024]{2,1,0:T(8,128)(2,1)S(1)} all-to-all(bf16[4,256,1024]{2,1,0:T(8,128)(2,1)S(1)} %bitcast.246), channel_id=1, replica_groups=mesh['seq'=64,'head'=4] {'head'}, dimensions={0} | all-to-all | bytes 4194304 | tf_op jit(solution)/shard_map/all_to_all | solution.py:162
  289.6 2.6 copy.124
  292.2 4.1 %copy.125 = bf16[256,4096]{1,0:T(8,128)(2,1)} copy(bf16[256,4096]{0,1:T(8,128)(2,1)} %bitcast.248) | data formatting | bytes 4194304 | tf_op jit(solution)/shard_map/all_to_all | solution.py:162
  (88 shorter events, 1.3 us)
Async XLA Ops:
  0.0 20.7 %copy-start = (bf16[1,256]{1,0:T(2,128)(2,1)S(1)}, bf16[1,256]{1,0:T(2,128)(2,1)}, u32[]{:S(2)}) copy-start(bf16[1,256]{1,0:T(2,128)(2,1)} %param.9) | copy-start | bytes 1540
  0.0 20.7 %copy-start.4 = (bf16[1024,128]{1,0:T(8,128)(2,1)S(1)}, bf16[1024,128]{1,0:T(8,128)(2,1)}, u32[]{:S(2)}) copy-start(bf16[1024,128]{1,0:T(8,128)(2,1)} %param.6) | copy-start | bytes 786436
  0.0 20.8 %copy-start.5 = (bf16[1024,128]{1,0:T(8,128)(2,1)S(1)}, bf16[1024,128]{1,0:T(8,128)(2,1)}, u32[]{:S(2)}) copy-start(bf16[1024,128]{1,0:T(8,128)(2,1)} %param.7) | copy-start | bytes 786436
  1.3 172.9 %collective-permute-start.2 = (bf16[128,128]{1,0:T(8,128)(2,1)S(1)}, bf16[128,128]{1,0:T(8,128)(2,1)S(1)}, u32[]{:S(2)}, u32[]{:S(2)}) collective-permute-start(bf16[128,128]{1,0:T(8,128)(2,1)S(1)} %convert_element_type.44), channel_id=1, source_target_pairs={{0,4},{4,8},{8,12},{12,16},{16,20},{20,24},{24,28},{28,32},{32,36}... | collective-permute-start | bytes 98312 | tf_op jit(solution)/shard_map/ppermute | solution.py:18
  6.1 176.0 %collective-permute-start.1 = (bf16[256,128]{1,0:T(8,128)(2,1)}, bf16[256,128]{1,0:T(8,128)(2,1)}, u32[]{:S(2)}, u32[]{:S(2)}) collective-permute-start(bf16[256,128]{1,0:T(8,128)(2,1)} %slice.249), channel_id=1, source_target_pairs={{0,4},{4,8},{8,12},{12,16},{16,20},{20,24},{24,28},{28,32},{32,36}... | collective-permute-start | bytes 196616 | tf_op jit(solution)/shard_map/ppermute | solution.py:18
  10.7 167.2 %collective-permute-start.5 = (bf16[128,128]{1,0:T(8,128)(2,1)S(1)}, bf16[128,128]{1,0:T(8,128)(2,1)S(1)}, u32[]{:S(2)}, u32[]{:S(2)}) collective-permute-start(bf16[128,128]{1,0:T(8,128)(2,1)S(1)} %convert_element_type.48), channel_id=1, source_target_pairs={{0,4},{4,8},{8,12},{12,16},{16,20},{20,24},{24,28},{28,32},{32,36}... | collective-permute-start | bytes 98312 | tf_op jit(solution)/shard_map/ppermute | solution.py:18
  15.3 183.5 %collective-permute-start = (bf16[256,128]{1,0:T(8,128)(2,1)}, bf16[256,128]{1,0:T(8,128)(2,1)}, u32[]{:S(2)}, u32[]{:S(2)}) collective-permute-start(bf16[256,128]{1,0:T(8,128)(2,1)} %slice.244), channel_id=1, source_target_pairs={{0,4},{4,8},{8,12},{12,16},{16,20},{20,24},{24,28},{28,32},{32,36}... | collective-permute-start | bytes 196616 | tf_op jit(solution)/shard_map/ppermute | solution.py:18
  174.2 18.7 %collective-permute-start.3 = (bf16[128,128]{1,0:T(8,128)(2,1)S(1)}, bf16[128,128]{1,0:T(8,128)(2,1)S(1)}, u32[]{:S(2)}, u32[]{:S(2)}) collective-permute-start(bf16[128,128]{1,0:T(8,128)(2,1)S(1)} %collective-permute-done.2), channel_id=1, source_target_pairs={{0,4},{4,8},{8,12},{12,16},{16,20},{20,24},{24,28},{28,32},{32,36}... | collective-permute-start | bytes 98312 | tf_op jit(solution)/shard_map/ppermute | solution.py:18
  177.9 23.5 %collective-permute-start.6 = (bf16[128,128]{1,0:T(8,128)(2,1)S(1)}, bf16[128,128]{1,0:T(8,128)(2,1)S(1)}, u32[]{:S(2)}, u32[]{:S(2)}) collective-permute-start(bf16[128,128]{1,0:T(8,128)(2,1)S(1)} %collective-permute-done.5), channel_id=1, source_target_pairs={{0,4},{4,8},{8,12},{12,16},{16,20},{20,24},{24,28},{28,32},{32,36}... | collective-permute-start | bytes 98312 | tf_op jit(solution)/shard_map/ppermute | solution.py:18
  192.9 17.4 %collective-permute-start.4 = (bf16[128,128]{1,0:T(8,128)(2,1)S(1)}, bf16[128,128]{1,0:T(8,128)(2,1)S(1)}, u32[]{:S(2)}, u32[]{:S(2)}) collective-permute-start(bf16[128,128]{1,0:T(8,128)(2,1)S(1)} %collective-permute-done.3), channel_id=1, source_target_pairs={{0,4},{4,8},{8,12},{12,16},{16,20},{20,24},{24,28},{28,32},{32,36}... | collective-permute-start | bytes 98312 | tf_op jit(solution)/shard_map/ppermute | solution.py:18
  201.5 10.6 %copy-start.3 = (f32[2,1,8,256,256]{3,4,2,0,1:T(8,128)S(1)}, f32[2,1,8,256,256]{3,4,2,0,1:T(8,128)}, u32[]{:S(2)}) copy-start(f32[2,1,8,256,256]{3,4,2,0,1:T(8,128)} %get-tuple-element.54) | copy-start | bytes 12582916
  201.5 21.3 %collective-permute-start.7 = (bf16[128,128]{1,0:T(8,128)(2,1)S(1)}, bf16[128,128]{1,0:T(8,128)(2,1)S(1)}, u32[]{:S(2)}, u32[]{:S(2)}) collective-permute-start(bf16[128,128]{1,0:T(8,128)(2,1)S(1)} %collective-permute-done.6), channel_id=1, source_target_pairs={{0,4},{4,8},{8,12},{12,16},{16,20},{20,24},{24,28},{28,32},{32,36}... | collective-permute-start | bytes 98312 | tf_op jit(solution)/shard_map/ppermute | solution.py:18
  211.1 6.7 %copy-start.13 = (bf16[2,256,1,128]{3,1,0,2:T(8,128)(2,1)}, bf16[2,256,1,128]{3,1,0,2:T(8,128)(2,1)S(1)}, u32[]{:S(2)}) copy-start(bf16[2,256,1,128]{3,1,0,2:T(8,128)(2,1)S(1)} %get-tuple-element.36) | copy-start | bytes 393220
  211.1 6.7 %slice-start.2 = ((s8[8388608]{0:T(1024)(128)(4,1)}), s8[4194304]{0:T(1024)(128)(4,1)S(1)}, s32[]{:S(2)}) async-start(s8[8388608]{0:T(1024)(128)(4,1)} %bitcast.238), calls=%async_computation.3 | async-start | bytes 8388608
  212.1 5.8 %slice-start.3 = ((s8[8388608]{0:T(1024)(128)(4,1)}), s8[4194304]{0:T(1024)(128)(4,1)S(1)}, s32[]{:S(2)}) async-start(s8[8388608]{0:T(1024)(128)(4,1)} %bitcast.238), calls=%async_computation.4 | async-start | bytes 8388608
  224.0 2.7 copy-start.7
  224.1 2.6 copy-start.9
  232.7 6.1 %copy-start.14 = (f32[2,8,256]{2,1,0:T(8,128)S(1)}, f32[2,8,256]{2,1,0:T(8,128)}, u32[]{:S(2)}) copy-start(f32[2,8,256]{2,1,0:T(8,128)} %get-tuple-element.47) | copy-start | bytes 49156
  232.7 6.1 %copy-start.15 = (f32[2,8,256]{2,1,0:T(8,128)S(1)}, f32[2,8,256]{2,1,0:T(8,128)}, u32[]{:S(2)}) copy-start(f32[2,8,256]{2,1,0:T(8,128)} %get-tuple-element.49) | copy-start | bytes 49156
  232.7 6.1 %copy-start.2 = (f32[2,1,8,256,256]{3,4,2,0,1:T(8,128)S(1)}, f32[2,1,8,256,256]{3,4,2,0,1:T(8,128)}, u32[]{:S(2)}) copy-start(f32[2,1,8,256,256]{3,4,2,0,1:T(8,128)} %get-tuple-element.48) | copy-start | bytes 12582916
  237.0 7.3 %slice-start = ((s8[8388608]{0:T(1024)(128)(4,1)}), s8[4194304]{0:T(1024)(128)(4,1)S(1)}, s32[]{:S(2)}) async-start(s8[8388608]{0:T(1024)(128)(4,1)} %bitcast.236), calls=%async_computation.1 | async-start | bytes 8388608
  238.8 5.5 %slice-start.1 = ((s8[8388608]{0:T(1024)(128)(4,1)}), s8[4194304]{0:T(1024)(128)(4,1)S(1)}, s32[]{:S(2)}) async-start(s8[8388608]{0:T(1024)(128)(4,1)} %bitcast.236), calls=%async_computation.2 | async-start | bytes 8388608
  244.3 5.0 %copy-start.17 = (bf16[64,128]{1,0:T(8,128)(2,1)S(1)}, bf16[64,128]{1,0:T(8,128)(2,1)}, u32[]{:S(2)}) copy-start(bf16[64,128]{1,0:T(8,128)(2,1)} %get-tuple-element.20) | copy-start | bytes 49156
  244.3 5.1 %copy-start.16 = (bf16[64,128]{1,0:T(8,128)(2,1)S(1)}, bf16[64,128]{1,0:T(8,128)(2,1)}, u32[]{:S(2)}) copy-start(bf16[64,128]{1,0:T(8,128)(2,1)} %get-tuple-element.21) | copy-start | bytes 49156
  244.3 5.2 %copy-start.8 = (bf16[2,32,1,128]{1,3,0,2:T(8,128)(2,1)S(1)}, bf16[2,32,1,128]{1,3,0,2:T(8,128)(2,1)}, u32[]{:S(2)}) copy-start(bf16[2,32,1,128]{1,3,0,2:T(8,128)(2,1)} %copy-done.7) | copy-start | bytes 49156
  244.3 5.2 %copy-start.10 = (bf16[2,32,1,128]{1,3,0,2:T(8,128)(2,1)S(1)}, bf16[2,32,1,128]{1,3,0,2:T(8,128)(2,1)}, u32[]{:S(2)}) copy-start(bf16[2,32,1,128]{1,3,0,2:T(8,128)(2,1)} %copy-done.9) | copy-start | bytes 49156
  249.3 2.6 copy-start.11
  249.3 2.6 copy-start.12
  254.8 3.4 %copy-start.6 = (bf16[64,8,8,128]{3,1,2,0:T(8,128)(2,1)S(1)}, bf16[64,8,8,128]{3,1,2,0:T(8,128)(2,1)}, u32[]{:S(2)}) copy-start(bf16[64,8,8,128]{3,1,2,0:T(8,128)(2,1)} %copy.178) | copy-start | bytes 3145732
  289.6 6.6 %copy-start.1 = (bf16[1,256]{1,0:T(2,128)(2,1)S(1)}, bf16[1,256]{1,0:T(2,128)(2,1)}, u32[]{:S(2)}) copy-start(bf16[1,256]{1,0:T(2,128)(2,1)} %param.9) | copy-start | bytes 1540
where the time goes:
time: 297 us; the launch traced here: 296 us
  blocking collectives  176 us (59%)
  matrix products  35.9 us (12%)
  starting transfers between devices  34.5 us (12%)
  other arithmetic  25.8 us (9%)
  local copies, waits for them, and re-layouts  23.7 us (8%)
    all_gather x1, blocking collectives, in_one_piece(): whole, at, outs = (lax.all_gather(both, axis, axis=dim, tiled=True), 0, [])  145 us
    ppermute x8, starting transfers between devices, passed_along(): return lax.ppermute(array, axis, pairs)  34.5 us
    all_to_all x1, blocking collectives, body(): lax.all_to_all(attended, 'head', split_axis=0, concat_axis=1, tiled=True)  31.2 us
    reduce_sum x2, other arithmetic, body(): row_total = jnp.sum(exponent, axis=-1, keepdims=True)  11.1 us
    dot_general x2, matrix products, body(): jnp.einsum('bqhsd,bkhd->bhsqk', query_rows, local_keys, preferred_element...  9.84 us
    convert_element_type x2, other arithmetic, body(): softmax_weights = (exponent / row_total).astype(jnp.bfloat16)  9.82 us
    unnamed x58, local copies, waits for them, and re-layouts  7.86 us
    all_to_all x2, local copies, waits for them, and re-layouts, body(): lax.all_to_all(attended, 'head', split_axis=0, concat_axis=1, tiled=True)  6.62 us
  transfers between devices with their start and end apart: 8, of which 0 were waited for; matrix products, arithmetic and copies ran while one was open for 14% of the time, Pallas kernels for 0%

commit v1 on v0

v1 whole, which is shorter than its diff:
```python
import math

import jax
import jax.numpy as jnp
from jax import lax
from jax.experimental import pallas as pl
from jax.experimental.pallas import tpu as pltpu
from jax.sharding import PartitionSpec as P

HEAD_DIM = 128
BLK = 256
GROUP = 8
PER = BLK // GROUP
MIDB = 8
MIDS = 256
HERE = 4
CLAN = 8
UNROLL = 4
MESH = pl.DeviceIdType.MESH
BF = jnp.bfloat16
F32 = jnp.float32
SCALE = math.log2(math.e) / math.sqrt(HEAD_DIM)


def nt(a, b):
    return lax.dot_general(a, b, (((1,), (1,)), ((), ())), preferred_element_type=F32)


def mm(a, b):
    return jnp.dot(a, b, preferred_element_type=F32)


def iota(shape, dim):
    return lax.broadcasted_iota(jnp.int32, shape, dim)


def pool_matrix(mid_ref, coarse_ref):
    row, col = iota((48, BLK), 0), iota((48, BLK), 1)
    mids = mid_ref[...].astype(F32)
    spread = jnp.zeros((1, BLK), F32)
    lane = iota((1, BLK), 1) % GROUP
    for t in range(GROUP):
        spread = jnp.where(lane == t, mids[0:1, t : t + 1], spread)
    w = jnp.where((row < PER) & (col // GROUP == row), spread, 0.0)
    return jnp.where(row == PER, coarse_ref[...].astype(F32), w).astype(BF)


def kernel(
    queries,
    keys,
    values,
    mid_pool,
    coarse_pool,
    out,
    qb,
    ob,
    near,
    mymid,
    mid,
    coarse,
    unit,
    in_sem,
    q_sem,
    halo_s,
    halo_r,
    one_s,
    one_r,
    two_s,
    two_r,
    out_s,
    out_r,
):
    s, h = lax.axis_index("seq"), lax.axis_index("head")
    devices = lax.axis_size("seq")
    clans = devices // CLAN
    a, b = s // CLAN, s % CLAN
    yh, core = h // 2, h % 2

    def target(i):
        fy, fc = 1 - i // 2, ((i + 1) // 2) % 2
        return ((yh + fy) % 2) * 2 + (core + fc) % 2

    loads = [
        pltpu.make_async_copy(keys, near.at[pl.ds(BLK, HERE * BLK), pl.ds(0, HEAD_DIM)], in_sem.at[0]),
        pltpu.make_async_copy(
            values, near.at[pl.ds(BLK, HERE * BLK), pl.ds(HEAD_DIM, HEAD_DIM)], in_sem.at[1]
        ),
    ]
    for c in loads:
        c.start()

    def q_load(i):
        return pltpu.make_async_copy(
            queries.at[pl.ds(pl.multiple_of(target(i) * BLK, BLK), BLK)], qb.at[i], q_sem.at[i]
        )

    for i in range(HERE):
        q_load(i).start()

    near[0:BLK, 0 : 2 * HEAD_DIM] = jnp.zeros((BLK, 2 * HEAD_DIM), BF)
    mid[0:288, 0 : 2 * HEAD_DIM] = jnp.zeros((288, 2 * HEAD_DIM), BF)
    coarse[:, 0 : 2 * HEAD_DIM] = jnp.zeros((coarse.shape[0], 2 * HEAD_DIM), BF)

    barrier = pltpu.get_barrier_semaphore()

    def tell(seq, head):
        pl.semaphore_signal(barrier, inc=1, device_id=(seq, head), device_id_type=MESH)

    for i in range(3):
        tell(s, target(i))
    for i in range(1, CLAN):
        tell(a * CLAN + (b + i) % CLAN, h)
    for back in (1, 2, 3):

        @pl.when(s >= back)
        def _():
            tell(s - back, h)

    def tell_lower(k, carry):
        tell(k * CLAN + b, h)
        return carry

    lax.fori_loop(0, a, tell_lower, 0)

    near[:, 2 * HEAD_DIM :] = jnp.ones((near.shape[0], HEAD_DIM), BF)
    mid[:, 2 * HEAD_DIM :] = jnp.ones((mid.shape[0], HEAD_DIM), BF)
    coarse[:, 2 * HEAD_DIM :] = jnp.ones((coarse.shape[0], HEAD_DIM), BF)
    pooling = pool_matrix(mid_pool, coarse_pool)
    for c in loads:
        c.wait()
    tops = []
    for j in range(HERE):
        pooled = mm(pooling, near[BLK + j * BLK : 2 * BLK + j * BLK, 0 : 2 * HEAD_DIM])
        mymid[j * PER : (j + 1) * PER, :] = pooled[0:PER].astype(BF)
        if j < 2:
            mid[288 + j * PER : 288 + (j + 1) * PER, 0 : 2 * HEAD_DIM] = pooled[0:PER].astype(BF)
        tops.append(pooled[PER : PER + 1])
    rows = [t[:, :HEAD_DIM] for t in tops] + [t[:, HEAD_DIM:] for t in tops]
    mine = jnp.zeros((16, HEAD_DIM), F32)
    for n, r in enumerate(rows):
        mine = jnp.where(iota((16, HEAD_DIM), 0) == n, r, mine)
    unit[b] = mine.astype(BF)

    pl.semaphore_wait(barrier, 3 + (CLAN - 1) + (clans - 1 - a) + jnp.minimum(3, devices - 1 - s))

    def one(i):
        return pltpu.make_async_remote_copy(
            src_ref=unit.at[b],
            dst_ref=unit.at[b],
            send_sem=one_s.at[i],
            recv_sem=one_r.at[i],
            device_id=(a * CLAN + (b + i) % CLAN, h),
            device_id_type=MESH,
        )

    def halo(n):
        src, dst, step = (
            (near.at[pl.ds(HERE * BLK, BLK), pl.ds(0, 256)], near.at[pl.ds(0, BLK), pl.ds(0, 256)], 1),
            (mymid, mid.at[pl.ds(160, 128), pl.ds(0, 256)], 1),
            (mymid, mid.at[pl.ds(32, 128), pl.ds(0, 256)], 2),
            (mymid.at[pl.ds(96, 32)], mid.at[pl.ds(0, 32), pl.ds(0, 256)], 3),
        )[n]
        copy = pltpu.make_async_remote_copy(
            src_ref=src,
            dst_ref=dst,
            send_sem=halo_s.at[n],
            recv_sem=halo_r.at[n],
            device_id=(s + step, h),
            device_id_type=MESH,
        )
        return copy, step

    def two(k):
        block = coarse.at[pl.ds(pl.multiple_of(a * 32, 32), 32), pl.ds(0, 256)]
        return pltpu.make_async_remote_copy(
            src_ref=block,
            dst_ref=block,
            send_sem=two_s.at[k],
            recv_sem=two_r.at[a],
            device_id=(k * CLAN + b, h),
            device_id_type=MESH,
        )

    def two_from(k):
        block = coarse.at[pl.ds(pl.multiple_of(k * 32, 32), 32), pl.ds(0, 256)]
        return pltpu.make_async_remote_copy(
            src_ref=block,
            dst_ref=block,
            send_sem=two_s.at[a],
            recv_sem=two_r.at[k],
            device_id=(k * CLAN + b, h),
            device_id_type=MESH,
        )

    for i in range(1, CLAN):
        one(i).start()
    for n in range(4):
        copy, step = halo(n)
        pl.when(s + step < devices)(copy.start)
    for i in range(1, CLAN):
        one(i).wait()
    units = unit[...].reshape(CLAN * 16, HEAD_DIM)
    r, c = iota((32, CLAN * 16), 0), iota((32, CLAN * 16), 1)
    at = (r // HERE) * 16 + r % HERE
    pick_k = jnp.where(c == at, 1.0, 0.0).astype(BF)
    pick_v = jnp.where(c == at + HERE, 1.0, 0.0).astype(BF)
    clan_rows = pl.ds(pl.multiple_of(a * 32, 32), 32)
    coarse[clan_rows, 0:HEAD_DIM] = mm(pick_k, units).astype(BF)
    coarse[clan_rows, HEAD_DIM : 2 * HEAD_DIM] = mm(pick_v, units).astype(BF)

    def start_two(k, carry):
        two(k).start()
        return carry

    lax.fori_loop(a + 1, clans, start_two, 0)
    for n in range(4):
        copy, step = halo(n)
        pl.when(s >= step)(copy.wait_recv)

    def got_two(k, carry):
        two_from(k).wait_recv()
        return carry

    lax.fori_loop(0, a, got_two, 0)
    for i in range(HERE):
        q_load(i).wait()

    wide = UNROLL * HEAD_DIM
    halves = qb.shape[2] // wide

    def sent(i, g):
        return pltpu.make_async_remote_copy(
            src_ref=ob.at[i, :, pl.ds(pl.multiple_of(g * wide, wide), wide)],
            dst_ref=out.at[:, pl.ds(pl.multiple_of(h * qb.shape[2] + g * wide, wide), wide)],
            send_sem=out_s.at[i, g],
            recv_sem=out_r.at[i, g],
            device_id=(s, target(i)),
            device_id_type=MESH,
        )

    def kept(g):
        return pltpu.make_async_copy(
            ob.at[3, :, pl.ds(pl.multiple_of(g * wide, wide), wide)],
            out.at[:, pl.ds(pl.multiple_of(h * qb.shape[2] + g * wide, wide), wide)],
            out_s.at[3, g],
        )

    causal = iota((BLK, BLK), 1) <= iota((BLK, BLK), 0)

    def step(t, carry):
        i, g = t // halves, t % halves
        j = target(i)
        block = s * HERE + j
        r0 = pl.multiple_of(j * BLK, BLK)
        m0 = pl.multiple_of(j * PER, PER)
        before = jnp.where(block >= 1, 0.0, -jnp.inf)
        mid_bias = jnp.where((block - 1 - MIDB) * PER + iota((1, MIDS), 1) >= 0, 0.0, -jnp.inf)
        coarse_bias = jnp.where(iota((1, coarse.shape[0]), 1) <= block - MIDB - 2, 0.0, -jnp.inf)
        for u in range(UNROLL):
            col = pl.multiple_of((g * UNROLL + u) * HEAD_DIM, HEAD_DIM)
            q = qb[i, :, pl.ds(col, HEAD_DIM)]
            s1 = nt(q, near[pl.ds(r0, BLK), 0:HEAD_DIM]) + before
            s2 = nt(q, near[pl.ds(r0 + BLK, BLK), 0:HEAD_DIM])
            s2 = jnp.where(causal, s2, -jnp.inf)
            s3 = nt(q, mid[pl.ds(m0, MIDS), 0:HEAD_DIM]) + mid_bias
            s4 = nt(q, coarse[:, 0:HEAD_DIM]) + coarse_bias
            top = jnp.maximum(jnp.maximum(s1, s2), jnp.maximum(s3, s4))
            top = jnp.max(top, axis=1, keepdims=True) * SCALE
            p1, p2, p3, p4 = [jnp.exp2(x * SCALE - top).astype(BF) for x in (s1, s2, s3, s4)]
            o = mm(p1, near[pl.ds(r0, BLK), HEAD_DIM:]) + mm(p2, near[pl.ds(r0 + BLK, BLK), HEAD_DIM:])
            o = o + mm(p3, mid[pl.ds(m0, MIDS), HEAD_DIM:]) + mm(p4, coarse[:, HEAD_DIM:])
            ob[i, :, pl.ds(col, HEAD_DIM)] = (o[:, :HEAD_DIM] / o[:, HEAD_DIM:]).astype(BF)

        @pl.when(i < 3)
        def _():
            sent(i, g).start()

        @pl.when(i == 3)
        def _():
            kept(g).start()

        return carry

    lax.fori_loop(0, HERE * halves, step, 0)

    for n in range(4):
        copy, step_up = halo(n)
        pl.when(s + step_up < devices)(copy.wait_send)

    def sent_two(k, carry):
        two(k).wait_send()
        return carry

    lax.fori_loop(a + 1, clans, sent_two, 0)
    for g in range(halves):
        for i in range(3):
            sent(i, g).wait()
        kept(g).wait()


def body(queries, keys, values, mid_pool, coarse_pool):
    rows, columns = queries.shape
    devices = lax.axis_size("seq")
    halves = columns // (UNROLL * HEAD_DIM)
    dma = pltpu.SemaphoreType.DMA
    any_, vmem = pl.BlockSpec(memory_space=pl.ANY), pl.BlockSpec(memory_space=pltpu.VMEM)
    return pl.pallas_call(
        kernel,
        out_shape=jax.ShapeDtypeStruct((rows // HERE, HERE * columns), BF),
        in_specs=[any_, any_, any_, vmem, vmem],
        out_specs=any_,
        scratch_shapes=[
            pltpu.VMEM((HERE, BLK, columns), BF),
            pltpu.VMEM((HERE, BLK, columns), BF),
            pltpu.VMEM(((HERE + 1) * BLK, 384), BF),
            pltpu.VMEM((HERE * PER, 256), BF),
            pltpu.VMEM((352, 384), BF),
            pltpu.VMEM((devices * HERE, 384), BF),
            pltpu.VMEM((CLAN, 16, HEAD_DIM), BF),
            dma((2,)),
            dma((HERE,)),
            dma((4,)),
            dma((4,)),
            dma((CLAN,)),
            dma((CLAN,)),
            dma((devices // CLAN,)),
            dma((devices // CLAN,)),
            dma((4, halves)),
            dma((3, halves)),
        ],
        compiler_params=pltpu.CompilerParams(
            collective_id=0, has_side_effects=True, vmem_limit_bytes=48 * 2**20
        ),
    )(queries, keys, values, mid_pool, coarse_pool)


def solution(mesh):
    return jax.shard_map(
        body,
        mesh=mesh,
        in_specs=(
            P("seq", "head"),
            P("seq", "head"),
            P("seq", "head"),
            P("head", None),
            P("head", None),
        ),
        out_specs=P(("seq", "head"), None),
        check_vma=False,
    )
```

time: 297 us -> 53 us (0.18)
  the two profiles are of different devices: /device:TPU:224 before, /device:TPU:31 now
where the time goes in v1:
time: 53 us; the launch traced here: 52.8 us
  Pallas kernels  46.6 us (88%)
  local copies, waits for them, and re-layouts  6.14 us (12%)
    pallas_call x1, Pallas kernels, body(): pl.pallas_call(kernel, out_shape=jax.ShapeDtypeStruct((rows // HERE, HERE...  46.6 us
    unnamed x11, local copies, waits for them, and re-layouts  6.14 us

profile of v1, /device:TPU:31, one launch (start us, length us, event | category | flops | bytes accessed | tf_op | source)
XLA Modules:
  0.0 52.8 jit_solution(15588113284897896796)
XLA Ops:
  0.0 0.0 copy-start
  0.0 1.6 %copy-done = bf16[1024,1024]{1,0:T(8,128)(2,1)S(1)} copy-done((bf16[1024,1024]{1,0:T(8,128)(2,1)S(1)}, bf16[1024,1024]{1,0:T(8,128)(2,1)}, u32[]{:S(2)}) %copy-start) | copy-done | bytes 2097176
  1.6 0.0 copy-start.1
  1.6 0.9 %copy-done.1 = bf16[1024,128]{1,0:T(8,128)(2,1)S(1)} copy-done((bf16[1024,128]{1,0:T(8,128)(2,1)S(1)}, bf16[1024,128]{1,0:T(8,128)(2,1)}, u32[]{:S(2)}) %copy-start.1) | copy-done | bytes 262168
  2.5 0.0 copy-start.2
  2.5 0.9 %copy-done.2 = bf16[1024,128]{1,0:T(8,128)(2,1)S(1)} copy-done((bf16[1024,128]{1,0:T(8,128)(2,1)S(1)}, bf16[1024,128]{1,0:T(8,128)(2,1)}, u32[]{:S(2)}) %copy-start.2) | copy-done | bytes 262168
  3.5 0.0 copy-start.3
  3.5 0.7 %copy-done.3 = bf16[1,256]{1,0:T(2,128)(2,1)S(1)} copy-done((bf16[1,256]{1,0:T(2,128)(2,1)S(1)}, bf16[1,256]{1,0:T(2,128)(2,1)}, u32[]{:S(2)}) %copy-start.3) | copy-done | bytes 536
  4.2 0.0 copy-start.4
  4.2 0.7 %copy-done.4 = bf16[1,8]{1,0:T(2,128)(2,1)S(1)} copy-done((bf16[1,8]{1,0:T(2,128)(2,1)S(1)}, bf16[1,8]{1,0:T(2,128)(2,1)}, u32[]{:S(2)}) %copy-start.4) | copy-done | bytes 40
  4.8 46.6 %shard_map.55 = bf16[256,4096]{1,0:T(8,128)(2,1)S(1)} custom-call(bf16[1024,1024]{1,0:T(8,128)(2,1)S(1)} %copy-done, bf16[1024,128]{1,0:T(8,128)(2,1)S(1)} %copy-done.1, bf16[1024,128]{1,0:T(8,128)(2,1)S(1)} %copy-done.2, bf16[1,8]{1,0:T(2,128)(2,1)S(1)} %copy-done.4, bf16[1,256]{1,0:T(2,128)(2,1)S(1)} %copy-done.3), custom_call_target="tpu_custom_call" | custom-call | tf_op jit(solution)/shard_map/pallas_call | solution.py:307
  51.5 1.3 %copy.7 = bf16[256,4096]{1,0:T(8,128)(2,1)} copy(bf16[256,4096]{1,0:T(8,128)(2,1)S(1)} %shard_map.55) | data formatting | bytes 4194304
Async XLA Ops:
  0.0 1.6 %copy-start = (bf16[1024,1024]{1,0:T(8,128)(2,1)S(1)}, bf16[1024,1024]{1,0:T(8,128)(2,1)}, u32[]{:S(2)}) copy-start(bf16[1024,1024]{1,0:T(8,128)(2,1)} %queries.1) | copy-start | bytes 6291460
  1.6 0.9 %copy-start.1 = (bf16[1024,128]{1,0:T(8,128)(2,1)S(1)}, bf16[1024,128]{1,0:T(8,128)(2,1)}, u32[]{:S(2)}) copy-start(bf16[1024,128]{1,0:T(8,128)(2,1)} %keys.1) | copy-start | bytes 786436
  2.5 0.9 %copy-start.2 = (bf16[1024,128]{1,0:T(8,128)(2,1)S(1)}, bf16[1024,128]{1,0:T(8,128)(2,1)}, u32[]{:S(2)}) copy-start(bf16[1024,128]{1,0:T(8,128)(2,1)} %values.1) | copy-start | bytes 786436
  3.5 0.7 %copy-start.3 = (bf16[1,256]{1,0:T(2,128)(2,1)S(1)}, bf16[1,256]{1,0:T(2,128)(2,1)}, u32[]{:S(2)}) copy-start(bf16[1,256]{1,0:T(2,128)(2,1)} %coarse_pool.1) | copy-start | bytes 1540
  4.2 0.7 %copy-start.4 = (bf16[1,8]{1,0:T(2,128)(2,1)S(1)}, bf16[1,8]{1,0:T(2,128)(2,1)}, u32[]{:S(2)}) copy-start(bf16[1,8]{1,0:T(2,128)(2,1)} %mid_pool.1) | copy-start | bytes 52

commit v2 on v1

--- a/solution.py
+++ b/solution.py
@@ -14,7 +14,9 @@
 MIDB = 8
 MIDS = 256
 HERE = 4
-CLAN = 8
+X, Z, Y = 4, 8, 2
+PLANE = X * Y
+ROWS = PLANE * HERE
 UNROLL = 4
 MESH = pl.DeviceIdType.MESH
 BF = jnp.bfloat16
@@ -59,6 +61,8 @@
     mid,
     coarse,
     unit,
+    mid_w,
+    coarse_w,
     in_sem,
     q_sem,
     halo_s,
@@ -67,14 +71,24 @@
     one_r,
     two_s,
     two_r,
+    ready_near,
+    ready_far,
     out_s,
     out_r,
 ):
     s, h = lax.axis_index("seq"), lax.axis_index("head")
     devices = lax.axis_size("seq")
-    clans = devices // CLAN
-    a, b = s // CLAN, s % CLAN
+    y, z, x = s // (Z * X), (s // X) % Z, s % X
+    u = y * X + x
     yh, core = h // 2, h % 2
+    early = z < Z // 2
+
+    def in_plane(i):
+        v = (u + i) % PLANE
+        return (v // X) * (Z * X) + z * X + v % X
+
+    def at_z(k):
+        return (y * Z + k) * X + x
 
     def target(i):
         fy, fc = 1 - i // 2, ((i + 1) // 2) % 2
@@ -85,6 +99,8 @@
         pltpu.make_async_copy(
             values, near.at[pl.ds(BLK, HERE * BLK), pl.ds(HEAD_DIM, HEAD_DIM)], in_sem.at[1]
         ),
+        pltpu.make_async_copy(mid_pool, mid_w, in_sem.at[2]),
+        pltpu.make_async_copy(coarse_pool, coarse_w, in_sem.at[3]),
     ]
     for c in loads:
         c.start()
@@ -94,13 +110,6 @@
             queries.at[pl.ds(pl.multiple_of(target(i) * BLK, BLK), BLK)], qb.at[i], q_sem.at[i]
         )
 
-    for i in range(HERE):
-        q_load(i).start()
-
-    near[0:BLK, 0 : 2 * HEAD_DIM] = jnp.zeros((BLK, 2 * HEAD_DIM), BF)
-    mid[0:288, 0 : 2 * HEAD_DIM] = jnp.zeros((288, 2 * HEAD_DIM), BF)
-    coarse[:, 0 : 2 * HEAD_DIM] = jnp.zeros((coarse.shape[0], 2 * HEAD_DIM), BF)
-
     barrier = pltpu.get_barrier_semaphore()
 
     def tell(seq, head):
@@ -108,26 +117,42 @@
 
     for i in range(3):
         tell(s, target(i))
-    for i in range(1, CLAN):
-        tell(a * CLAN + (b + i) % CLAN, h)
+    for i in range(1, PLANE):
+        tell(in_plane(i), h)
     for back in (1, 2, 3):
 
         @pl.when(s >= back)
         def _():
             tell(s - back, h)
 
-    def tell_lower(k, carry):
-        tell(k * CLAN + b, h)
-        return carry
-
-    lax.fori_loop(0, a, tell_lower, 0)
+    def tell_upper(k, carry):
+        tell(at_z(k), h)
+        return carry
+
+    lax.fori_loop(z + 1, Z, tell_upper, 0)
+
+    def blank(ref, start, size):
+        ref[pl.ds(start, size), 0 : 2 * HEAD_DIM] = jnp.zeros((size, 2 * HEAD_DIM), BF)
+
+    pl.when(s < 1)(lambda: blank(near, 0, BLK))
+    pl.when(s < 1)(lambda: blank(mid, 160, 128))
+    pl.when(s < 2)(lambda: blank(mid, 32, 128))
+    pl.when(s < 3)(lambda: blank(mid, 0, 32))
+
+    def blank_coarse(k, carry):
+        blank(coarse, pl.multiple_of(k * ROWS, ROWS), ROWS)
+        return carry
+
+    lax.fori_loop(jnp.where(y == 0, z + 1, Z), Z, blank_coarse, 0)
 
     near[:, 2 * HEAD_DIM :] = jnp.ones((near.shape[0], HEAD_DIM), BF)
     mid[:, 2 * HEAD_DIM :] = jnp.ones((mid.shape[0], HEAD_DIM), BF)
     coarse[:, 2 * HEAD_DIM :] = jnp.ones((coarse.shape[0], HEAD_DIM), BF)
-    pooling = pool_matrix(mid_pool, coarse_pool)
     for c in loads:
         c.wait()
+    for i in range(HERE):
+        q_load(i).start()
+    pooling = pool_matrix(mid_w, coarse_w)
     tops = []
     for j in range(HERE):
         pooled = mm(pooling, near[BLK + j * BLK : 2 * BLK + j * BLK, 0 : 2 * HEAD_DIM])
@@ -139,26 +164,38 @@
     mine = jnp.zeros((16, HEAD_DIM), F32)
     for n, r in enumerate(rows):
         mine = jnp.where(iota((16, HEAD_DIM), 0) == n, r, mine)
-    unit[b] = mine.astype(BF)
-
-    pl.semaphore_wait(barrier, 3 + (CLAN - 1) + (clans - 1 - a) + jnp.minimum(3, devices - 1 - s))
+    unit[u] = mine.astype(BF)
+
+    pl.semaphore_wait(barrier, 3 + (PLANE - 1) + z + jnp.minimum(3, devices - 1 - s))
+
+    half = z - z % (Z // 2)
+
+    def tell_ready(sem):
+        def tell_one(k, carry):
+            pl.semaphore_signal(sem, inc=1, device_id=(at_z(k), h), device_id_type=MESH)
+            return carry
+
+        return tell_one
+
+    lax.fori_loop(half, z, tell_ready(ready_near), 0)
+    lax.fori_loop(0, half, tell_ready(ready_far), 0)
 
     def one(i):
         return pltpu.make_async_remote_copy(
-            src_ref=unit.at[b],
-            dst_ref=unit.at[b],
-            send_sem=one_s.at[i],
-            recv_sem=one_r.at[i],
-            device_id=(a * CLAN + (b + i) % CLAN, h),
+            src_ref=unit.at[u],
+            dst_ref=unit.at[u],
+            send_sem=one_s,
+            recv_sem=one_r,
+            device_id=(in_plane(i), h),
             device_id_type=MESH,
         )
 
     def halo(n):
         src, dst, step = (
-            (near.at[pl.ds(HERE * BLK, BLK), pl.ds(0, 256)], near.at[pl.ds(0, BLK), pl.ds(0, 256)], 1),
             (mymid, mid.at[pl.ds(160, 128), pl.ds(0, 256)], 1),
             (mymid, mid.at[pl.ds(32, 128), pl.ds(0, 256)], 2),
             (mymid.at[pl.ds(96, 32)], mid.at[pl.ds(0, 32), pl.ds(0, 256)], 3),
+            (near.at[pl.ds(HERE * BLK, BLK), pl.ds(0, 256)], near.at[pl.ds(0, BLK), pl.ds(0, 256)], 1),
         )[n]
         copy = pltpu.make_async_remote_copy(
             src_ref=src,
@@ -170,58 +207,71 @@
         )
         return copy, step
 
-    def two(k):
-        block = coarse.at[pl.ds(pl.multiple_of(a * 32, 32), 32), pl.ds(0, 256)]
+    def plane_rows(k):
+        return pl.ds(pl.multiple_of(k * ROWS, ROWS), ROWS)
+
+    def two(k, of):
+        block = coarse.at[plane_rows(of), pl.ds(0, 256)]
         return pltpu.make_async_remote_copy(
             src_ref=block,
             dst_ref=block,
             send_sem=two_s.at[k],
-            recv_sem=two_r.at[a],
-            device_id=(k * CLAN + b, h),
+            recv_sem=two_r.at[of],
+            device_id=(at_z(k), h),
             device_id_type=MESH,
         )
 
-    def two_from(k):
-        block = coarse.at[pl.ds(pl.multiple_of(k * 32, 32), 32), pl.ds(0, 256)]
-        return pltpu.make_async_remote_copy(
-            src_ref=block,
-            dst_ref=block,
-            send_sem=two_s.at[a],
-            recv_sem=two_r.at[k],
-            device_id=(k * CLAN + b, h),
-            device_id_type=MESH,
-        )
-
-    for i in range(1, CLAN):
+    for i in range(1, PLANE):
         one(i).start()
-    for n in range(4):
+    for n in range(3):
         copy, step = halo(n)
         pl.when(s + step < devices)(copy.start)
-    for i in range(1, CLAN):
-        one(i).wait()
-    units = unit[...].reshape(CLAN * 16, HEAD_DIM)
-    r, c = iota((32, CLAN * 16), 0), iota((32, CLAN * 16), 1)
+    others = unit.at[pl.ds(0, PLANE - 1)]
+    all_ones = pltpu.make_async_remote_copy(
+        src_ref=others,
+        dst_ref=others,
+        send_sem=one_s,
+        recv_sem=one_r,
+        device_id=(in_plane(1), h),
+        device_id_type=MESH,
+    )
+    all_ones.wait_recv()
+    units = unit[...].reshape(PLANE * 16, HEAD_DIM)
+    r, c = iota((ROWS, PLANE * 16), 0), iota((ROWS, PLANE * 16), 1)
     at = (r // HERE) * 16 + r % HERE
     pick_k = jnp.where(c == at, 1.0, 0.0).astype(BF)
     pick_v = jnp.where(c == at + HERE, 1.0, 0.0).astype(BF)
-    clan_rows = pl.ds(pl.multiple_of(a * 32, 32), 32)
-    coarse[clan_rows, 0:HEAD_DIM] = mm(pick_k, units).astype(BF)
-    coarse[clan_rows, HEAD_DIM : 2 * HEAD_DIM] = mm(pick_v, units).astype(BF)
+    coarse[plane_rows(z), 0:HEAD_DIM] = mm(pick_k, units).astype(BF)
+    coarse[plane_rows(z), HEAD_DIM : 2 * HEAD_DIM] = mm(pick_v, units).astype(BF)
 
     def start_two(k, carry):
-        two(k).start()
-        return carry
-
-    lax.fori_loop(a + 1, clans, start_two, 0)
+        two(k, z).start()
+        return carry
+
+    low = jnp.where(y == 1, 0, z)
+    lax.fori_loop(low, z, start_two, 0)
+    above = half + Z // 2 - 1 - z
+    pl.when(above > 0)(lambda: pl.semaphore_wait(ready_near, above))
+    lax.fori_loop(z + 1, half + Z // 2, start_two, 0)
+
+    def send_far():
+        pl.semaphore_wait(ready_far, Z // 2)
+        lax.fori_loop(Z // 2, Z, start_two, 0)
+
+    first = early & (y == 0) & (z < 2)
+    pl.when(early & jnp.logical_not(first))(send_far)
+    tail, _ = halo(3)
+    pl.when(s + 1 < devices)(tail.start)
     for n in range(4):
         copy, step = halo(n)
         pl.when(s >= step)(copy.wait_recv)
 
     def got_two(k, carry):
-        two_from(k).wait_recv()
-        return carry
-
-    lax.fori_loop(0, a, got_two, 0)
+        two(z, k).wait_recv()
+        return carry
+
+    lax.fori_loop(0, z, got_two, 0)
+    lax.fori_loop(z + 1, jnp.where(y == 1, Z, z + 1), got_two, 0)
     for i in range(HERE):
         q_load(i).wait()
 
@@ -255,7 +305,9 @@
         m0 = pl.multiple_of(j * PER, PER)
         before = jnp.where(block >= 1, 0.0, -jnp.inf)
         mid_bias = jnp.where((block - 1 - MIDB) * PER + iota((1, MIDS), 1) >= 0, 0.0, -jnp.inf)
-        coarse_bias = jnp.where(iota((1, coarse.shape[0]), 1) <= block - MIDB - 2, 0.0, -jnp.inf)
+        p = iota((1, coarse.shape[0]), 1)
+        c = (p // (X * HERE)) % Y * (Z * X * HERE) + p // ROWS * (X * HERE) + p % (X * HERE)
+        coarse_bias = jnp.where(c <= block - MIDB - 2, 0.0, -jnp.inf)
         for u in range(UNROLL):
             col = pl.multiple_of((g * UNROLL + u) * HEAD_DIM, HEAD_DIM)
             q = qb[i, :, pl.ds(col, HEAD_DIM)]
@@ -279,6 +331,7 @@
         def _():
             kept(g).start()
 
+        pl.when((t == 0) & first)(send_far)
         return carry
 
     lax.fori_loop(0, HERE * halves, step, 0)
@@ -288,10 +341,12 @@
         pl.when(s + step_up < devices)(copy.wait_send)
 
     def sent_two(k, carry):
-        two(k).wait_send()
-        return carry
-
-    lax.fori_loop(a + 1, clans, sent_two, 0)
+        two(k, z).wait_send()
+        return carry
+
+    lax.fori_loop(low, z, sent_two, 0)
+    lax.fori_loop(z + 1, Z, sent_two, 0)
+    all_ones.wait_send()
     for g in range(halves):
         for i in range(3):
             sent(i, g).wait()
@@ -303,11 +358,11 @@
     devices = lax.axis_size("seq")
     halves = columns // (UNROLL * HEAD_DIM)
     dma = pltpu.SemaphoreType.DMA
-    any_, vmem = pl.BlockSpec(memory_space=pl.ANY), pl.BlockSpec(memory_space=pltpu.VMEM)
+    hbm, any_ = pl.BlockSpec(memory_space=pltpu.HBM), pl.BlockSpec(memory_space=pl.ANY)
     return pl.pallas_call(
         kernel,
         out_shape=jax.ShapeDtypeStruct((rows // HERE, HERE * columns), BF),
-        in_specs=[any_, any_, any_, vmem, vmem],
+        in_specs=[hbm] * 5,
         out_specs=any_,
         scratch_shapes=[
             pltpu.VMEM((HERE, BLK, columns), BF),
@@ -316,20 +371,24 @@
             pltpu.VMEM((HERE * PER, 256), BF),
             pltpu.VMEM((352, 384), BF),
             pltpu.VMEM((devices * HERE, 384), BF),
-            pltpu.VMEM((CLAN, 16, HEAD_DIM), BF),
-            dma((2,)),
+            pltpu.VMEM((PLANE, 16, HEAD_DIM), BF),
+            pltpu.VMEM((1, GROUP), BF),
+            pltpu.VMEM((1, BLK), BF),
+            dma((4,)),
             dma((HERE,)),
             dma((4,)),
             dma((4,)),
-            dma((CLAN,)),
-            dma((CLAN,)),
-            dma((devices // CLAN,)),
-            dma((devices // CLAN,)),
+            dma,
+            dma,
+            dma((Z,)),
+            dma((Z,)),
+            pltpu.SemaphoreType.REGULAR,
+            pltpu.SemaphoreType.REGULAR,
             dma((4, halves)),
             dma((3, halves)),
         ],
         compiler_params=pltpu.CompilerParams(
-            collective_id=0, has_side_effects=True, vmem_limit_bytes=48 * 2**20
+            collective_id=0, has_side_effects=True, vmem_limit_bytes=60 * 2**20
         ),
     )(queries, keys, values, mid_pool, coarse_pool)
 

time: 53 us -> 47.8 us (0.902)
  the two profiles are of different devices: /device:TPU:31 before, /device:TPU:161 now
where the time goes in v2:
time: 47.8 us; the launch traced here: 47.7 us
  Pallas kernels  44.6 us (93%)
  local copies, waits for them, and re-layouts  3.13 us (7%)
    pallas_call x1, Pallas kernels, body(): pl.pallas_call(kernel, out_shape=jax.ShapeDtypeStruct((rows // HERE, HERE...  44.6 us
    unnamed x1, local copies, waits for them, and re-layouts  3.13 us

profile of v2, /device:TPU:161, one launch (start us, length us, event | category | flops | bytes accessed | tf_op | source)
XLA Modules:
  0.0 47.7 jit_solution(8648621151956608155)
XLA Ops:
  0.0 44.6 %shard_map.55 = bf16[256,4096]{1,0:T(8,128)(2,1)} custom-call(bf16[1024,1024]{1,0:T(8,128)(2,1)} %queries.1, bf16[1024,128]{1,0:T(8,128)(2,1)} %keys.1, bf16[1024,128]{1,0:T(8,128)(2,1)} %values.1, bf16[1,8]{1,0:T(2,128)(2,1)} %mid_pool.1, bf16[1,256]{1,0:T(2,128)(2,1)} %coarse_pool.1), custom_call_target="tpu_custom_call" | custom-call | tf_op jit(solution)/shard_map/pallas_call | solution.py:362
  44.6 3.1 %copy.7 = bf16[256,4096]{1,0:T(8,128)(2,1)} copy(bf16[256,4096]{1,0:T(8,128)(2,1)} %shard_map.55) | data formatting | bytes 4194304

commit v3 on v2

--- a/solution.py
+++ b/solution.py
@@ -73,6 +73,8 @@
     two_r,
     ready_near,
     ready_far,
+    ctx_s,
+    ctx_r,
     out_s,
     out_r,
 ):
@@ -90,14 +92,24 @@
     def at_z(k):
         return (y * Z + k) * X + x
 
-    def target(i):
-        fy, fc = 1 - i // 2, ((i + 1) // 2) % 2
-        return ((yh + fy) % 2) * 2 + (core + fc) % 2
+    gives = (core == 1) & (y == 1)
+    partner = h + 2 - 4 * yh
+
+    def block_of(i):
+        n = jnp.where(y == 1, jnp.where(i == 3, 3, (i + 2) % 3), i)
+        there, here = (1 - yh) * 2 + (1 - n % 2), yh * 2 + (core + n + 1) % 2
+        return jnp.where(gives, yh * 2 + i % 2, jnp.where(n < 2, there, here))
+
+    def context_of(i):
+        return jnp.where(gives, i // 2, 0)
+
+    def heads_of(i):
+        return jnp.where(gives & (i >= 2), partner, h)
 
     loads = [
-        pltpu.make_async_copy(keys, near.at[pl.ds(BLK, HERE * BLK), pl.ds(0, HEAD_DIM)], in_sem.at[0]),
+        pltpu.make_async_copy(keys, near.at[0, pl.ds(BLK, HERE * BLK), pl.ds(0, HEAD_DIM)], in_sem.at[0]),
         pltpu.make_async_copy(
-            values, near.at[pl.ds(BLK, HERE * BLK), pl.ds(HEAD_DIM, HEAD_DIM)], in_sem.at[1]
+            values, near.at[0, pl.ds(BLK, HERE * BLK), pl.ds(HEAD_DIM, HEAD_DIM)], in_sem.at[1]
         ),
         pltpu.make_async_copy(mid_pool, mid_w, in_sem.at[2]),
         pltpu.make_async_copy(coarse_pool, coarse_w, in_sem.at[3]),
@@ -107,7 +119,7 @@
 
     def q_load(i):
         return pltpu.make_async_copy(
-            queries.at[pl.ds(pl.multiple_of(target(i) * BLK, BLK), BLK)], qb.at[i], q_sem.at[i]
+            queries.at[pl.ds(pl.multiple_of(block_of(i) * BLK, BLK), BLK)], qb.at[i], q_sem.at[i]
         )
 
     barrier = pltpu.get_barrier_semaphore()
@@ -115,8 +127,8 @@
     def tell(seq, head):
         pl.semaphore_signal(barrier, inc=1, device_id=(seq, head), device_id_type=MESH)
 
-    for i in range(3):
-        tell(s, target(i))
+    for i in range(1, 4):
+        tell(s, (h + i) % 4)
     for i in range(1, PLANE):
         tell(in_plane(i), h)
     for back in (1, 2, 3):
@@ -132,7 +144,7 @@
     lax.fori_loop(z + 1, Z, tell_upper, 0)
 
     def blank(ref, start, size):
-        ref[pl.ds(start, size), 0 : 2 * HEAD_DIM] = jnp.zeros((size, 2 * HEAD_DIM), BF)
+        ref[0, pl.ds(start, size), 0 : 2 * HEAD_DIM] = jnp.zeros((size, 2 * HEAD_DIM), BF)
 
     pl.when(s < 1)(lambda: blank(near, 0, BLK))
     pl.when(s < 1)(lambda: blank(mid, 160, 128))
@@ -145,20 +157,20 @@
 
     lax.fori_loop(jnp.where(y == 0, z + 1, Z), Z, blank_coarse, 0)
 
-    near[:, 2 * HEAD_DIM :] = jnp.ones((near.shape[0], HEAD_DIM), BF)
-    mid[:, 2 * HEAD_DIM :] = jnp.ones((mid.shape[0], HEAD_DIM), BF)
-    coarse[:, 2 * HEAD_DIM :] = jnp.ones((coarse.shape[0], HEAD_DIM), BF)
+    for ref in (near, mid, coarse):
+        for k in range(2):
+            ref[k, :, 2 * HEAD_DIM :] = jnp.ones((ref.shape[1], HEAD_DIM), BF)
     for c in loads:
         c.wait()
     for i in range(HERE):
-        q_load(i).start()
+        pl.when(jnp.logical_not(gives) | (i < 2))(q_load(i).start)
     pooling = pool_matrix(mid_w, coarse_w)
     tops = []
     for j in range(HERE):
-        pooled = mm(pooling, near[BLK + j * BLK : 2 * BLK + j * BLK, 0 : 2 * HEAD_DIM])
+        pooled = mm(pooling, near[0, BLK + j * BLK : 2 * BLK + j * BLK, 0 : 2 * HEAD_DIM])
         mymid[j * PER : (j + 1) * PER, :] = pooled[0:PER].astype(BF)
         if j < 2:
-            mid[288 + j * PER : 288 + (j + 1) * PER, 0 : 2 * HEAD_DIM] = pooled[0:PER].astype(BF)
+            mid[0, 288 + j * PER : 288 + (j + 1) * PER, 0 : 2 * HEAD_DIM] = pooled[0:PER].astype(BF)
         tops.append(pooled[PER : PER + 1])
     rows = [t[:, :HEAD_DIM] for t in tops] + [t[:, HEAD_DIM:] for t in tops]
     mine = jnp.zeros((16, HEAD_DIM), F32)
@@ -192,10 +204,14 @@
 
     def halo(n):
         src, dst, step = (
-            (mymid, mid.at[pl.ds(160, 128), pl.ds(0, 256)], 1),
-            (mymid, mid.at[pl.ds(32, 128), pl.ds(0, 256)], 2),
-            (mymid.at[pl.ds(96, 32)], mid.at[pl.ds(0, 32), pl.ds(0, 256)], 3),
-            (near.at[pl.ds(HERE * BLK, BLK), pl.ds(0, 256)], near.at[pl.ds(0, BLK), pl.ds(0, 256)], 1),
+            (mymid, mid.at[0, pl.ds(160, 128), pl.ds(0, 256)], 1),
+            (mymid, mid.at[0, pl.ds(32, 128), pl.ds(0, 256)], 2),
+            (mymid.at[pl.ds(96, 32)], mid.at[0, pl.ds(0, 32), pl.ds(0, 256)], 3),
+            (
+                near.at[0, pl.ds(HERE * BLK, BLK), pl.ds(0, 256)],
+                near.at[0, pl.ds(0, BLK), pl.ds(0, 256)],
+                1,
+            ),
         )[n]
         copy = pltpu.make_async_remote_copy(
             src_ref=src,
@@ -207,11 +223,31 @@
         )
         return copy, step
 
+    def give(n):
+        away = 1 - yh
+        even = pl.multiple_of(away * 2 * BLK, 2 * BLK)
+        src, dst = (
+            (queries.at[pl.ds(even, BLK)], qb.at[2]),
+            (queries.at[pl.ds(even + BLK, BLK)], qb.at[3]),
+            tuple(near.at[k, pl.ds(even + BLK, 2 * BLK), pl.ds(0, 256)] for k in (0, 1)),
+            tuple(near.at[k, pl.ds(even, BLK), pl.ds(0, 256)] for k in (0, 1)),
+            tuple(mid.at[k, pl.ds(pl.multiple_of(away * 64, 64), 288), pl.ds(0, 256)] for k in (0, 1)),
+            tuple(coarse.at[k, :, pl.ds(0, 256)] for k in (0, 1)),
+        )[n]
+        return pltpu.make_async_remote_copy(
+            src_ref=src,
+            dst_ref=dst,
+            send_sem=ctx_s.at[n],
+            recv_sem=ctx_r.at[n],
+            device_id=(s, partner),
+            device_id_type=MESH,
+        )
+
     def plane_rows(k):
         return pl.ds(pl.multiple_of(k * ROWS, ROWS), ROWS)
 
     def two(k, of):
-        block = coarse.at[plane_rows(of), pl.ds(0, 256)]
+        block = coarse.at[0, plane_rows(of), pl.ds(0, 256)]
         return pltpu.make_async_remote_copy(
             src_ref=block,
             dst_ref=block,
@@ -226,6 +262,8 @@
     for n in range(3):
         copy, step = halo(n)
         pl.when(s + step < devices)(copy.start)
+    for n in (2, 0, 1):
+        pl.when(gives)(give(n).start)
     others = unit.at[pl.ds(0, PLANE - 1)]
     all_ones = pltpu.make_async_remote_copy(
         src_ref=others,
@@ -241,8 +279,8 @@
     at = (r // HERE) * 16 + r % HERE
     pick_k = jnp.where(c == at, 1.0, 0.0).astype(BF)
     pick_v = jnp.where(c == at + HERE, 1.0, 0.0).astype(BF)
-    coarse[plane_rows(z), 0:HEAD_DIM] = mm(pick_k, units).astype(BF)
-    coarse[plane_rows(z), HEAD_DIM : 2 * HEAD_DIM] = mm(pick_v, units).astype(BF)
+    coarse[0, plane_rows(z), 0:HEAD_DIM] = mm(pick_k, units).astype(BF)
+    coarse[0, plane_rows(z), HEAD_DIM : 2 * HEAD_DIM] = mm(pick_v, units).astype(BF)
 
     def start_two(k, carry):
         two(k, z).start()
@@ -262,7 +300,7 @@
     pl.when(early & jnp.logical_not(first))(send_far)
     tail, _ = halo(3)
     pl.when(s + 1 < devices)(tail.start)
-    for n in range(4):
+    for n in range(3):
         copy, step = halo(n)
         pl.when(s >= step)(copy.wait_recv)
 
@@ -273,63 +311,87 @@
     lax.fori_loop(0, z, got_two, 0)
     lax.fori_loop(z + 1, jnp.where(y == 1, Z, z + 1), got_two, 0)
     for i in range(HERE):
-        q_load(i).wait()
+        pl.when(jnp.logical_not(gives) | (i < 2))(q_load(i).wait)
+    pl.when(gives & (s >= 1))(tail.wait_recv)
+    for n in (4, 5, 3):
+        pl.when(gives)(give(n).start)
 
     wide = UNROLL * HEAD_DIM
     halves = qb.shape[2] // wide
+
+    def columns_of(head, g):
+        return pl.ds(pl.multiple_of(head * qb.shape[2] + g * wide, wide), wide)
 
     def sent(i, g):
         return pltpu.make_async_remote_copy(
             src_ref=ob.at[i, :, pl.ds(pl.multiple_of(g * wide, wide), wide)],
-            dst_ref=out.at[:, pl.ds(pl.multiple_of(h * qb.shape[2] + g * wide, wide), wide)],
+            dst_ref=out.at[:, columns_of(heads_of(i), g)],
             send_sem=out_s.at[i, g],
-            recv_sem=out_r.at[i, g],
-            device_id=(s, target(i)),
+            recv_sem=out_r.at[heads_of(i), g],
+            device_id=(s, block_of(i)),
             device_id_type=MESH,
         )
 
-    def kept(g):
+    def arriving(source, g):
+        block = out.at[:, columns_of(source, g)]
+        return pltpu.make_async_remote_copy(
+            src_ref=block,
+            dst_ref=block,
+            send_sem=out_s.at[0, g],
+            recv_sem=out_r.at[source, g],
+            device_id=(s, source),
+            device_id_type=MESH,
+        )
+
+    def kept(i, g):
         return pltpu.make_async_copy(
-            ob.at[3, :, pl.ds(pl.multiple_of(g * wide, wide), wide)],
-            out.at[:, pl.ds(pl.multiple_of(h * qb.shape[2] + g * wide, wide), wide)],
-            out_s.at[3, g],
+            ob.at[i, :, pl.ds(pl.multiple_of(g * wide, wide), wide)],
+            out.at[:, columns_of(heads_of(i), g)],
+            out_s.at[i, g],
         )
 
     causal = iota((BLK, BLK), 1) <= iota((BLK, BLK), 0)
 
     def step(t, carry):
         i, g = t // halves, t % halves
-        j = target(i)
+        j, k = block_of(i), context_of(i)
         block = s * HERE + j
+        pl.when((j == 0) & (g == 0) & (s >= 1) & jnp.logical_not(gives))(tail.wait_recv)
+
+        @pl.when(gives & (t == 2 * halves))
+        def _():
+            for n in range(6):
+                give(n).wait_recv()
+
         r0 = pl.multiple_of(j * BLK, BLK)
         m0 = pl.multiple_of(j * PER, PER)
         before = jnp.where(block >= 1, 0.0, -jnp.inf)
         mid_bias = jnp.where((block - 1 - MIDB) * PER + iota((1, MIDS), 1) >= 0, 0.0, -jnp.inf)
-        p = iota((1, coarse.shape[0]), 1)
+        p = iota((1, coarse.shape[1]), 1)
         c = (p // (X * HERE)) % Y * (Z * X * HERE) + p // ROWS * (X * HERE) + p % (X * HERE)
         coarse_bias = jnp.where(c <= block - MIDB - 2, 0.0, -jnp.inf)
         for u in range(UNROLL):
             col = pl.multiple_of((g * UNROLL + u) * HEAD_DIM, HEAD_DIM)
             q = qb[i, :, pl.ds(col, HEAD_DIM)]
-            s1 = nt(q, near[pl.ds(r0, BLK), 0:HEAD_DIM]) + before
-            s2 = nt(q, near[pl.ds(r0 + BLK, BLK), 0:HEAD_DIM])
+            s1 = nt(q, near[k, pl.ds(r0, BLK), 0:HEAD_DIM]) + before
+            s2 = nt(q, near[k, pl.ds(r0 + BLK, BLK), 0:HEAD_DIM])
             s2 = jnp.where(causal, s2, -jnp.inf)
-            s3 = nt(q, mid[pl.ds(m0, MIDS), 0:HEAD_DIM]) + mid_bias
-            s4 = nt(q, coarse[:, 0:HEAD_DIM]) + coarse_bias
+            s3 = nt(q, mid[k, pl.ds(m0, MIDS), 0:HEAD_DIM]) + mid_bias
+            s4 = nt(q, coarse[k, :, 0:HEAD_DIM]) + coarse_bias
             top = jnp.maximum(jnp.maximum(s1, s2), jnp.maximum(s3, s4))
             top = jnp.max(top, axis=1, keepdims=True) * SCALE
             p1, p2, p3, p4 = [jnp.exp2(x * SCALE - top).astype(BF) for x in (s1, s2, s3, s4)]
-            o = mm(p1, near[pl.ds(r0, BLK), HEAD_DIM:]) + mm(p2, near[pl.ds(r0 + BLK, BLK), HEAD_DIM:])
-            o = o + mm(p3, mid[pl.ds(m0, MIDS), HEAD_DIM:]) + mm(p4, coarse[:, HEAD_DIM:])
+            o = mm(p1, near[k, pl.ds(r0, BLK), HEAD_DIM:]) + mm(p2, near[k, pl.ds(r0 + BLK, BLK), HEAD_DIM:])
+            o = o + mm(p3, mid[k, pl.ds(m0, MIDS), HEAD_DIM:]) + mm(p4, coarse[k, :, HEAD_DIM:])
             ob[i, :, pl.ds(col, HEAD_DIM)] = (o[:, :HEAD_DIM] / o[:, HEAD_DIM:]).astype(BF)
 
-        @pl.when(i < 3)
+        @pl.when(j != h)
         def _():
             sent(i, g).start()
 
-        @pl.when(i == 3)
+        @pl.when(j == h)
         def _():
-            kept(g).start()
+            kept(i, g).start()
 
         pl.when((t == 0) & first)(send_far)
         return carry
@@ -347,10 +409,29 @@
     lax.fori_loop(low, z, sent_two, 0)
     lax.fori_loop(z + 1, Z, sent_two, 0)
     all_ones.wait_send()
+    for n in range(6):
+        pl.when(gives)(give(n).wait_send)
     for g in range(halves):
-        for i in range(3):
-            sent(i, g).wait()
-        kept(g).wait()
+        for i in range(HERE):
+            pl.when(block_of(i) != h)(sent(i, g).wait_send)
+            pl.when(block_of(i) == h)(kept(i, g).wait)
+        for d in (1, 2, 3):
+            other = (h + d) % 4
+            pl.when(jnp.logical_not(gives) | (d != 2))(arriving(other, g).wait_recv)
+
+
+def settle(src, dst, buf, sem):
+    n, rows = 16, src.shape[0] // 16
+    parts = [pl.ds(i * rows, rows) for i in range(n)]
+    ins = [pltpu.make_async_copy(src.at[p], buf.at[p], sem.at[0, i]) for i, p in enumerate(parts)]
+    outs = [pltpu.make_async_copy(buf.at[p], dst.at[p], sem.at[1, i]) for i, p in enumerate(parts)]
+    for c in ins:
+        c.start()
+    for a, b in zip(ins, outs):
+        a.wait()
+        b.start()
+    for b in outs:
+        b.wait()
 
 
 def body(queries, keys, values, mid_pool, coarse_pool):
@@ -359,7 +440,7 @@
     halves = columns // (UNROLL * HEAD_DIM)
     dma = pltpu.SemaphoreType.DMA
     hbm, any_ = pl.BlockSpec(memory_space=pltpu.HBM), pl.BlockSpec(memory_space=pl.ANY)
-    return pl.pallas_call(
+    landed = pl.pallas_call(
         kernel,
         out_shape=jax.ShapeDtypeStruct((rows // HERE, HERE * columns), BF),
         in_specs=[hbm] * 5,
@@ -367,10 +448,10 @@
         scratch_shapes=[
             pltpu.VMEM((HERE, BLK, columns), BF),
             pltpu.VMEM((HERE, BLK, columns), BF),
-            pltpu.VMEM(((HERE + 1) * BLK, 384), BF),
+            pltpu.VMEM((2, (HERE + 1) * BLK, 384), BF),
             pltpu.VMEM((HERE * PER, 256), BF),
-            pltpu.VMEM((352, 384), BF),
-            pltpu.VMEM((devices * HERE, 384), BF),
+            pltpu.VMEM((2, 352, 384), BF),
+            pltpu.VMEM((2, devices * HERE, 384), BF),
             pltpu.VMEM((PLANE, 16, HEAD_DIM), BF),
             pltpu.VMEM((1, GROUP), BF),
             pltpu.VMEM((1, BLK), BF),
@@ -384,13 +465,23 @@
             dma((Z,)),
             pltpu.SemaphoreType.REGULAR,
             pltpu.SemaphoreType.REGULAR,
+            dma((6,)),
+            dma((6,)),
+            dma((HERE, halves)),
             dma((4, halves)),
-            dma((3, halves)),
         ],
         compiler_params=pltpu.CompilerParams(
             collective_id=0, has_side_effects=True, vmem_limit_bytes=60 * 2**20
         ),
     )(queries, keys, values, mid_pool, coarse_pool)
+    return pl.pallas_call(
+        settle,
+        out_shape=jax.ShapeDtypeStruct(landed.shape, BF),
+        in_specs=[any_],
+        out_specs=any_,
+        scratch_shapes=[pltpu.VMEM(landed.shape, BF), dma((2, 16))],
+        compiler_params=pltpu.CompilerParams(vmem_limit_bytes=60 * 2**20),
+    )(landed)
 
 
 def solution(mesh):

time: 47.8 us -> 43.4 us (0.908)
  the two profiles are of different devices: /device:TPU:161 before, /device:TPU:198 now
where the time goes in v3:
time: 43.4 us; the launch traced here: 43.2 us
  Pallas kernels  43.2 us (100%)
    pallas_call x1, Pallas kernels, body(): pl.pallas_call(kernel, out_shape=jax.ShapeDtypeStruct((rows // HERE, HERE...  40.6 us
    pallas_call x1, Pallas kernels, body(): pl.pallas_call(settle, out_shape=jax.ShapeDtypeStruct(landed.shape, BF),...  2.57 us

profile of v3, /device:TPU:198, one launch (start us, length us, event | category | flops | bytes accessed | tf_op | source)
XLA Modules:
  0.0 43.2 jit_solution(15787392325640572321)
XLA Ops:
  0.0 40.6 %shard_map.55.src = bf16[256,4096]{1,0:T(8,128)(2,1)} custom-call(bf16[1024,1024]{1,0:T(8,128)(2,1)} %queries.1, bf16[1024,128]{1,0:T(8,128)(2,1)} %keys.1, bf16[1024,128]{1,0:T(8,128)(2,1)} %values.1, bf16[1,8]{1,0:T(2,128)(2,1)} %mid_pool.1, bf16[1,256]{1,0:T(2,128)(2,1)} %coarse_pool.1), custom_call_target="tpu_custom_call" | custom-call | tf_op jit(solution)/shard_map/pallas_call | solution.py:443
  40.7 2.6 %shard_map.56 = bf16[256,4096]{1,0:T(8,128)(2,1)} custom-call(bf16[256,4096]{1,0:T(8,128)(2,1)} %shard_map.55.src), custom_call_target="tpu_custom_call" | custom-call | tf_op jit(solution)/shard_map/pallas_call | solution.py:477

commit v4 on v3

--- a/solution.py
+++ b/solution.py
@@ -56,6 +56,8 @@
     out,
     qb,
     ob,
+    half_o,
+    half_m,
     near,
     mymid,
     mid,
@@ -92,19 +94,26 @@
     def at_z(k):
         return (y * Z + k) * X + x
 
-    gives = (core == 1) & (y == 1)
+    gives = (core == 1) & (s > 0)
+    both = gives & (y == 1)
+    taken = jnp.where(gives, 3 - y, HERE)
     partner = h + 2 - 4 * yh
 
     def block_of(i):
-        n = jnp.where(y == 1, jnp.where(i == 3, 3, (i + 2) % 3), i)
-        there, here = (1 - yh) * 2 + (1 - n % 2), yh * 2 + (core + n + 1) % 2
-        return jnp.where(gives, yh * 2 + i % 2, jnp.where(n < 2, there, here))
+        odd, even = (1 - yh) * 2 + 1, (1 - yh) * 2
+        other, own = yh * 2 + 1 - core, yh * 2 + core
+
+        def pick(*blocks):
+            return jnp.where(i == 0, blocks[0], jnp.where(i == 1, blocks[1], jnp.where(i == 2, blocks[2], blocks[3])))
+
+        giving = jnp.where(y == 1, pick(own, other, other, own), pick(odd, other, own, other))
+        return jnp.where(gives, giving, jnp.where(y == 1, pick(other, odd, even, own), pick(odd, even, other, own)))
 
     def context_of(i):
-        return jnp.where(gives, i // 2, 0)
+        return jnp.where(i >= taken, 1, 0)
 
     def heads_of(i):
-        return jnp.where(gives & (i >= 2), partner, h)
+        return jnp.where(i >= taken, partner, h)
 
     loads = [
         pltpu.make_async_copy(keys, near.at[0, pl.ds(BLK, HERE * BLK), pl.ds(0, HEAD_DIM)], in_sem.at[0]),
@@ -147,6 +156,7 @@
         ref[0, pl.ds(start, size), 0 : 2 * HEAD_DIM] = jnp.zeros((size, 2 * HEAD_DIM), BF)
 
     pl.when(s < 1)(lambda: blank(near, 0, BLK))
+    pl.when(s < 1)(lambda: blank(coarse, 0, ROWS))
     pl.when(s < 1)(lambda: blank(mid, 160, 128))
     pl.when(s < 2)(lambda: blank(mid, 32, 128))
     pl.when(s < 3)(lambda: blank(mid, 0, 32))
@@ -163,7 +173,7 @@
     for c in loads:
         c.wait()
     for i in range(HERE):
-        pl.when(jnp.logical_not(gives) | (i < 2))(q_load(i).start)
+        pl.when(i < taken)(q_load(i).start)
     pooling = pool_matrix(mid_w, coarse_w)
     tops = []
     for j in range(HERE):
@@ -227,12 +237,13 @@
         away = 1 - yh
         even = pl.multiple_of(away * 2 * BLK, 2 * BLK)
         src, dst = (
-            (queries.at[pl.ds(even, BLK)], qb.at[2]),
+            (queries.at[pl.ds(even, BLK)], qb.at[jnp.where(both, 2, 3)]),
             (queries.at[pl.ds(even + BLK, BLK)], qb.at[3]),
-            tuple(near.at[k, pl.ds(even + BLK, 2 * BLK), pl.ds(0, 256)] for k in (0, 1)),
+            tuple(near.at[k, pl.ds(even + BLK, BLK), pl.ds(0, 256)] for k in (0, 1)),
             tuple(near.at[k, pl.ds(even, BLK), pl.ds(0, 256)] for k in (0, 1)),
             tuple(mid.at[k, pl.ds(pl.multiple_of(away * 64, 64), 288), pl.ds(0, 256)] for k in (0, 1)),
             tuple(coarse.at[k, :, pl.ds(0, 256)] for k in (0, 1)),
+            tuple(near.at[k, pl.ds(even + 2 * BLK, BLK), pl.ds(0, 256)] for k in (0, 1)),
         )[n]
         return pltpu.make_async_remote_copy(
             src_ref=src,
@@ -262,8 +273,119 @@
     for n in range(3):
         copy, step = halo(n)
         pl.when(s + step < devices)(copy.start)
-    for n in (2, 0, 1):
+    tail, _ = halo(3)
+    pl.when(s + 1 < devices)(tail.start)
+    for n in (2, 0):
         pl.when(gives)(give(n).start)
+    for n in (6, 1):
+        pl.when(both)(give(n).start)
+    def start_two(k, carry):
+        two(k, z).start()
+        return carry
+
+    def send_far():
+        pl.semaphore_wait(ready_far, Z // 2)
+        lax.fori_loop(Z // 2, Z, start_two, 0)
+
+    first = early & (y == 0) & (z < 2)
+    causal = iota((BLK, BLK), 1) <= iota((BLK, BLK), 0)
+    own0 = pl.multiple_of(block_of(0) * BLK, BLK)
+
+    def near_step(g, carry):
+        for u in range(UNROLL):
+            col = pl.multiple_of((g * UNROLL + u) * HEAD_DIM, HEAD_DIM)
+            col2 = pl.multiple_of((g * UNROLL + u) * 2 * HEAD_DIM, 2 * HEAD_DIM)
+            q = qb[0, :, pl.ds(col, HEAD_DIM)]
+            s1 = nt(q, near[0, pl.ds(own0, BLK), 0:HEAD_DIM])
+            s2 = nt(q, near[0, pl.ds(own0 + BLK, BLK), 0:HEAD_DIM])
+            s2 = jnp.where(causal, s2, -jnp.inf)
+            top = jnp.max(jnp.maximum(s1, s2), axis=1, keepdims=True) * SCALE
+            p1, p2 = [jnp.exp2(x * SCALE - top).astype(BF) for x in (s1, s2)]
+            o = mm(p1, near[0, pl.ds(own0, BLK), HEAD_DIM:]) + mm(p2, near[0, pl.ds(own0 + BLK, BLK), HEAD_DIM:])
+            half_o[:, pl.ds(col2, 2 * HEAD_DIM)] = o
+            half_m[:, pl.ds(col, HEAD_DIM)] = jnp.broadcast_to(top, (BLK, HEAD_DIM))
+        return carry
+
+    wide = UNROLL * HEAD_DIM
+    halves = qb.shape[2] // wide
+
+    def columns_of(head, g):
+        return pl.ds(pl.multiple_of(head * qb.shape[2] + g * wide, wide), wide)
+
+    def sent(i, g):
+        return pltpu.make_async_remote_copy(
+            src_ref=ob.at[i, :, pl.ds(pl.multiple_of(g * wide, wide), wide)],
+            dst_ref=out.at[:, columns_of(heads_of(i), g)],
+            send_sem=out_s.at[i, g],
+            recv_sem=out_r.at[heads_of(i), g],
+            device_id=(s, block_of(i)),
+            device_id_type=MESH,
+        )
+
+    def arriving(source, g):
+        block = out.at[:, columns_of(source, g)]
+        return pltpu.make_async_remote_copy(
+            src_ref=block,
+            dst_ref=block,
+            send_sem=out_s.at[0, g],
+            recv_sem=out_r.at[source, g],
+            device_id=(s, source),
+            device_id_type=MESH,
+        )
+
+    def kept(i, g):
+        return pltpu.make_async_copy(
+            ob.at[i, :, pl.ds(pl.multiple_of(g * wide, wide), wide)],
+            out.at[:, columns_of(heads_of(i), g)],
+            out_s.at[i, g],
+        )
+
+    def mid_bias_of(block):
+        return jnp.where((block - 1 - MIDB) * PER + iota((1, MIDS), 1) >= 0, 0.0, -jnp.inf)
+
+    def coarse_bias_of(block):
+        p = iota((1, coarse.shape[1]), 1)
+        c = (p // (X * HERE)) % Y * (Z * X * HERE) + p // ROWS * (X * HERE) + p % (X * HERE)
+        return jnp.where(c <= block - MIDB - 2, 0.0, -jnp.inf)
+
+    def deliver(i, g):
+        @pl.when(block_of(i) != h)
+        def _():
+            sent(i, g).start()
+
+        @pl.when(block_of(i) == h)
+        def _():
+            kept(i, g).start()
+
+    def first_step(g, carry):
+        block = s * HERE + block_of(0)
+        m0 = pl.multiple_of(block_of(0) * PER, PER)
+        mid_bias, coarse_bias = mid_bias_of(block), coarse_bias_of(block)
+        for u in range(UNROLL):
+            col = pl.multiple_of((g * UNROLL + u) * HEAD_DIM, HEAD_DIM)
+            col2 = pl.multiple_of((g * UNROLL + u) * 2 * HEAD_DIM, 2 * HEAD_DIM)
+            q = qb[0, :, pl.ds(col, HEAD_DIM)]
+            s3 = nt(q, mid[0, pl.ds(m0, MIDS), 0:HEAD_DIM]) + mid_bias
+            s4 = nt(q, coarse[0, :, 0:HEAD_DIM]) + coarse_bias
+            before = half_m[:, pl.ds(col, HEAD_DIM)][:, 0:1]
+            top = jnp.maximum(jnp.max(jnp.maximum(s3, s4), axis=1, keepdims=True) * SCALE, before)
+            p3, p4 = [jnp.exp2(x * SCALE - top).astype(BF) for x in (s3, s4)]
+            o = half_o[:, pl.ds(col2, 2 * HEAD_DIM)] * jnp.exp2(before - top)
+            o = o + mm(p3, mid[0, pl.ds(m0, MIDS), HEAD_DIM:]) + mm(p4, coarse[0, :, HEAD_DIM:])
+            ob[0, :, pl.ds(col, HEAD_DIM)] = (o[:, :HEAD_DIM] / o[:, HEAD_DIM:]).astype(BF)
+        deliver(0, g)
+        pl.when((g == 0) & first & (s > 0))(send_far)
+        return carry
+
+    def near_part():
+        q_load(0).wait()
+        lax.fori_loop(0, halves, near_step, 0)
+
+    @pl.when(s == 0)
+    def _():
+        near_part()
+        lax.fori_loop(0, halves, first_step, 0)
+
     others = unit.at[pl.ds(0, PLANE - 1)]
     all_ones = pltpu.make_async_remote_copy(
         src_ref=others,
@@ -282,24 +404,15 @@
     coarse[0, plane_rows(z), 0:HEAD_DIM] = mm(pick_k, units).astype(BF)
     coarse[0, plane_rows(z), HEAD_DIM : 2 * HEAD_DIM] = mm(pick_v, units).astype(BF)
 
-    def start_two(k, carry):
-        two(k, z).start()
-        return carry
-
     low = jnp.where(y == 1, 0, z)
     lax.fori_loop(low, z, start_two, 0)
     above = half + Z // 2 - 1 - z
     pl.when(above > 0)(lambda: pl.semaphore_wait(ready_near, above))
     lax.fori_loop(z + 1, half + Z // 2, start_two, 0)
 
-    def send_far():
-        pl.semaphore_wait(ready_far, Z // 2)
-        lax.fori_loop(Z // 2, Z, start_two, 0)
-
-    first = early & (y == 0) & (z < 2)
     pl.when(early & jnp.logical_not(first))(send_far)
-    tail, _ = halo(3)
-    pl.when(s + 1 < devices)(tail.start)
+
+    pl.when(s > 0)(near_part)
     for n in range(3):
         copy, step = halo(n)
         pl.when(s >= step)(copy.wait_recv)
@@ -310,47 +423,18 @@
 
     lax.fori_loop(0, z, got_two, 0)
     lax.fori_loop(z + 1, jnp.where(y == 1, Z, z + 1), got_two, 0)
-    for i in range(HERE):
-        pl.when(jnp.logical_not(gives) | (i < 2))(q_load(i).wait)
+    for i in range(1, HERE):
+        pl.when(i < taken)(q_load(i).wait)
+    for n in (4, 5):
+        pl.when(gives)(give(n).start)
     pl.when(gives & (s >= 1))(tail.wait_recv)
-    for n in (4, 5, 3):
-        pl.when(gives)(give(n).start)
-
-    wide = UNROLL * HEAD_DIM
-    halves = qb.shape[2] // wide
-
-    def columns_of(head, g):
-        return pl.ds(pl.multiple_of(head * qb.shape[2] + g * wide, wide), wide)
-
-    def sent(i, g):
-        return pltpu.make_async_remote_copy(
-            src_ref=ob.at[i, :, pl.ds(pl.multiple_of(g * wide, wide), wide)],
-            dst_ref=out.at[:, columns_of(heads_of(i), g)],
-            send_sem=out_s.at[i, g],
-            recv_sem=out_r.at[heads_of(i), g],
-            device_id=(s, block_of(i)),
-            device_id_type=MESH,
-        )
-
-    def arriving(source, g):
-        block = out.at[:, columns_of(source, g)]
-        return pltpu.make_async_remote_copy(
-            src_ref=block,
-            dst_ref=block,
-            send_sem=out_s.at[0, g],
-            recv_sem=out_r.at[source, g],
-            device_id=(s, source),
-            device_id_type=MESH,
-        )
-
-    def kept(i, g):
-        return pltpu.make_async_copy(
-            ob.at[i, :, pl.ds(pl.multiple_of(g * wide, wide), wide)],
-            out.at[:, columns_of(heads_of(i), g)],
-            out_s.at[i, g],
-        )
-
-    causal = iota((BLK, BLK), 1) <= iota((BLK, BLK), 0)
+    pl.when(gives)(give(3).start)
+
+    @pl.when(s > 0)
+    def _():
+        lax.fori_loop(0, halves, first_step, 0)
+
+    pl.when(s == 0)(send_far)
 
     def step(t, carry):
         i, g = t // halves, t % halves
@@ -358,18 +442,17 @@
         block = s * HERE + j
         pl.when((j == 0) & (g == 0) & (s >= 1) & jnp.logical_not(gives))(tail.wait_recv)
 
-        @pl.when(gives & (t == 2 * halves))
+        @pl.when(t == taken * halves)
         def _():
-            for n in range(6):
+            for n in (0, 2, 3, 4, 5):
                 give(n).wait_recv()
 
+        pl.when(both & (t == 2 * halves))(give(6).wait_recv)
+        pl.when(both & (t == 3 * halves))(give(1).wait_recv)
         r0 = pl.multiple_of(j * BLK, BLK)
         m0 = pl.multiple_of(j * PER, PER)
         before = jnp.where(block >= 1, 0.0, -jnp.inf)
-        mid_bias = jnp.where((block - 1 - MIDB) * PER + iota((1, MIDS), 1) >= 0, 0.0, -jnp.inf)
-        p = iota((1, coarse.shape[1]), 1)
-        c = (p // (X * HERE)) % Y * (Z * X * HERE) + p // ROWS * (X * HERE) + p % (X * HERE)
-        coarse_bias = jnp.where(c <= block - MIDB - 2, 0.0, -jnp.inf)
+        mid_bias, coarse_bias = mid_bias_of(block), coarse_bias_of(block)
         for u in range(UNROLL):
             col = pl.multiple_of((g * UNROLL + u) * HEAD_DIM, HEAD_DIM)
             q = qb[i, :, pl.ds(col, HEAD_DIM)]
@@ -385,18 +468,10 @@
             o = o + mm(p3, mid[k, pl.ds(m0, MIDS), HEAD_DIM:]) + mm(p4, coarse[k, :, HEAD_DIM:])
             ob[i, :, pl.ds(col, HEAD_DIM)] = (o[:, :HEAD_DIM] / o[:, HEAD_DIM:]).astype(BF)
 
-        @pl.when(j != h)
-        def _():
-            sent(i, g).start()
-
-        @pl.when(j == h)
-        def _():
-            kept(i, g).start()
-
-        pl.when((t == 0) & first)(send_far)
-        return carry
-
-    lax.fori_loop(0, HERE * halves, step, 0)
+        deliver(i, g)
+        return carry
+
+    lax.fori_loop(halves, HERE * halves, step, 0)
 
     for n in range(4):
         copy, step_up = halo(n)
@@ -409,15 +484,17 @@
     lax.fori_loop(low, z, sent_two, 0)
     lax.fori_loop(z + 1, Z, sent_two, 0)
     all_ones.wait_send()
-    for n in range(6):
+    for n in (0, 2, 3, 4, 5):
         pl.when(gives)(give(n).wait_send)
+    for n in (1, 6):
+        pl.when(both)(give(n).wait_send)
     for g in range(halves):
         for i in range(HERE):
             pl.when(block_of(i) != h)(sent(i, g).wait_send)
             pl.when(block_of(i) == h)(kept(i, g).wait)
         for d in (1, 2, 3):
             other = (h + d) % 4
-            pl.when(jnp.logical_not(gives) | (d != 2))(arriving(other, g).wait_recv)
+            pl.when(jnp.logical_not(both) | (d != 2))(arriving(other, g).wait_recv)
 
 
 def settle(src, dst, buf, sem):
@@ -448,6 +525,8 @@
         scratch_shapes=[
             pltpu.VMEM((HERE, BLK, columns), BF),
             pltpu.VMEM((HERE, BLK, columns), BF),
+            pltpu.VMEM((BLK, 2 * columns), F32),
+            pltpu.VMEM((BLK, columns), F32),
             pltpu.VMEM((2, (HERE + 1) * BLK, 384), BF),
             pltpu.VMEM((HERE * PER, 256), BF),
             pltpu.VMEM((2, 352, 384), BF),
@@ -465,8 +544,8 @@
             dma((Z,)),
             pltpu.SemaphoreType.REGULAR,
             pltpu.SemaphoreType.REGULAR,
-            dma((6,)),
-            dma((6,)),
+            dma((7,)),
+            dma((7,)),
             dma((HERE, halves)),
             dma((4, halves)),
         ],

time: 43.4 us -> 42 us (0.968); the launches traced: 43.2 us -> 41.1 us
  Pallas kernels: 43.2 us -> 41.1 us
    pallas_call x1, Pallas kernels: 40.6 us -> 38.6 us  [body(): pl.pallas_call(kernel, out_shape=jax.ShapeDtypeStruct((rows // HERE, HERE...]
where the time goes in v4:
time: 42 us; the launch traced here: 41.1 us
  Pallas kernels  41.1 us (98%)
    pallas_call x1, Pallas kernels, body(): pl.pallas_call(kernel, out_shape=jax.ShapeDtypeStruct((rows // HERE, HERE...  38.6 us
    pallas_call x1, Pallas kernels, body(): pl.pallas_call(settle, out_shape=jax.ShapeDtypeStruct(landed.shape, BF),...  2.57 us

profile of v4, /device:TPU:198, one launch (start us, length us, event | category | flops | bytes accessed | tf_op | source)
XLA Modules:
  0.0 41.1 jit_solution(12760655726862629593)
XLA Ops:
  0.0 38.6 %shard_map.55.src = bf16[256,4096]{1,0:T(8,128)(2,1)} custom-call(bf16[1024,1024]{1,0:T(8,128)(2,1)} %queries.1, bf16[1024,128]{1,0:T(8,128)(2,1)} %keys.1, bf16[1024,128]{1,0:T(8,128)(2,1)} %values.1, bf16[1,8]{1,0:T(2,128)(2,1)} %mid_pool.1, bf16[1,256]{1,0:T(2,128)(2,1)} %coarse_pool.1), custom_call_target="tpu_custom_call" | custom-call | tf_op jit(solution)/shard_map/pallas_call | solution.py:520
  38.6 2.6 %shard_map.56 = bf16[256,4096]{1,0:T(8,128)(2,1)} custom-call(bf16[256,4096]{1,0:T(8,128)(2,1)} %shard_map.55.src), custom_call_target="tpu_custom_call" | custom-call | tf_op jit(solution)/shard_map/pallas_call | solution.py:556

commit v5 on v4

--- a/solution.py
+++ b/solution.py
@@ -103,11 +103,13 @@
         odd, even = (1 - yh) * 2 + 1, (1 - yh) * 2
         other, own = yh * 2 + 1 - core, yh * 2 + core
 
+        late = (y == 1) & (z >= 2)
+
         def pick(*blocks):
             return jnp.where(i == 0, blocks[0], jnp.where(i == 1, blocks[1], jnp.where(i == 2, blocks[2], blocks[3])))
 
         giving = jnp.where(y == 1, pick(own, other, other, own), pick(odd, other, own, other))
-        return jnp.where(gives, giving, jnp.where(y == 1, pick(other, odd, even, own), pick(odd, even, other, own)))
+        return jnp.where(gives, giving, jnp.where(late, pick(other, odd, even, own), jnp.where(y == 1, pick(odd, other, even, own), pick(odd, even, other, own))))
 
     def context_of(i):
         return jnp.where(i >= taken, 1, 0)
@@ -498,7 +500,7 @@
 
 
 def settle(src, dst, buf, sem):
-    n, rows = 16, src.shape[0] // 16
+    n, rows = 8, src.shape[0] // 8
     parts = [pl.ds(i * rows, rows) for i in range(n)]
     ins = [pltpu.make_async_copy(src.at[p], buf.at[p], sem.at[0, i]) for i, p in enumerate(parts)]
     outs = [pltpu.make_async_copy(buf.at[p], dst.at[p], sem.at[1, i]) for i, p in enumerate(parts)]
@@ -558,7 +560,7 @@
         out_shape=jax.ShapeDtypeStruct(landed.shape, BF),
         in_specs=[any_],
         out_specs=any_,
-        scratch_shapes=[pltpu.VMEM(landed.shape, BF), dma((2, 16))],
+        scratch_shapes=[pltpu.VMEM(landed.shape, BF), dma((2, 8))],
         compiler_params=pltpu.CompilerParams(vmem_limit_bytes=60 * 2**20),
     )(landed)
 

time: 42 us -> 41.1 us (0.979); the launches traced: 41.1 us -> 41 us
  no operation moved by 1% of the time
where the time goes in v5:
time: 41.1 us; the launch traced here: 41 us
  Pallas kernels  40.9 us (100%)
    pallas_call x1, Pallas kernels, body(): pl.pallas_call(kernel, out_shape=jax.ShapeDtypeStruct((rows // HERE, HERE...  38.6 us
    pallas_call x1, Pallas kernels, body(): pl.pallas_call(settle, out_shape=jax.ShapeDtypeStruct(landed.shape, BF),...  2.4 us

profile of v5, /device:TPU:198, one launch (start us, length us, event | category | flops | bytes accessed | tf_op | source)
XLA Modules:
  0.0 41.0 jit_solution(6197798758347643762)
XLA Ops:
  0.0 38.6 %shard_map.55.src = bf16[256,4096]{1,0:T(8,128)(2,1)} custom-call(bf16[1024,1024]{1,0:T(8,128)(2,1)} %queries.1, bf16[1024,128]{1,0:T(8,128)(2,1)} %keys.1, bf16[1024,128]{1,0:T(8,128)(2,1)} %values.1, bf16[1,8]{1,0:T(2,128)(2,1)} %mid_pool.1, bf16[1,256]{1,0:T(2,128)(2,1)} %coarse_pool.1), custom_call_target="tpu_custom_call" | custom-call | tf_op jit(solution)/shard_map/pallas_call | solution.py:522
  38.6 2.4 %shard_map.56 = bf16[256,4096]{1,0:T(8,128)(2,1)} custom-call(bf16[256,4096]{1,0:T(8,128)(2,1)} %shard_map.55.src), custom_call_target="tpu_custom_call" | custom-call | tf_op jit(solution)/shard_map/pallas_call | solution.py:558

commit v6 on v5

--- a/solution.py
+++ b/solution.py
@@ -159,6 +159,12 @@
 
     pl.when(s < 1)(lambda: blank(near, 0, BLK))
     pl.when(s < 1)(lambda: blank(coarse, 0, ROWS))
+
+    @pl.when(y == 0)
+    def _():
+        for k in range(Z):
+            half = pl.ds(k * ROWS + X * HERE, ROWS - X * HERE)
+            coarse[1, half, 0 : 2 * HEAD_DIM] = jnp.zeros((ROWS - X * HERE, 2 * HEAD_DIM), BF)
     pl.when(s < 1)(lambda: blank(mid, 160, 128))
     pl.when(s < 2)(lambda: blank(mid, 32, 128))
     pl.when(s < 3)(lambda: blank(mid, 0, 32))
@@ -246,6 +252,7 @@
             tuple(mid.at[k, pl.ds(pl.multiple_of(away * 64, 64), 288), pl.ds(0, 256)] for k in (0, 1)),
             tuple(coarse.at[k, :, pl.ds(0, 256)] for k in (0, 1)),
             tuple(near.at[k, pl.ds(even + 2 * BLK, BLK), pl.ds(0, 256)] for k in (0, 1)),
+            tuple(coarse.reshape(2, Z, ROWS, 384).at[k, :, pl.ds(0, X * HERE), pl.ds(0, 256)] for k in (0, 1)),
         )[n]
         return pltpu.make_async_remote_copy(
             src_ref=src,
@@ -427,8 +434,9 @@
     lax.fori_loop(z + 1, jnp.where(y == 1, Z, z + 1), got_two, 0)
     for i in range(1, HERE):
         pl.when(i < taken)(q_load(i).wait)
-    for n in (4, 5):
-        pl.when(gives)(give(n).start)
+    pl.when(gives)(give(4).start)
+    pl.when(both)(give(5).start)
+    pl.when(gives & (y == 0))(give(7).start)
     pl.when(gives & (s >= 1))(tail.wait_recv)
     pl.when(gives)(give(3).start)
 
@@ -446,8 +454,10 @@
 
         @pl.when(t == taken * halves)
         def _():
-            for n in (0, 2, 3, 4, 5):
+            for n in (0, 2, 3, 4):
                 give(n).wait_recv()
+            pl.when(y == 1)(give(5).wait_recv)
+            pl.when(y == 0)(give(7).wait_recv)
 
         pl.when(both & (t == 2 * halves))(give(6).wait_recv)
         pl.when(both & (t == 3 * halves))(give(1).wait_recv)
@@ -486,10 +496,11 @@
     lax.fori_loop(low, z, sent_two, 0)
     lax.fori_loop(z + 1, Z, sent_two, 0)
     all_ones.wait_send()
-    for n in (0, 2, 3, 4, 5):
+    for n in (0, 2, 3, 4):
         pl.when(gives)(give(n).wait_send)
-    for n in (1, 6):
+    for n in (1, 5, 6):
         pl.when(both)(give(n).wait_send)
+    pl.when(gives & (y == 0))(give(7).wait_send)
     for g in range(halves):
         for i in range(HERE):
             pl.when(block_of(i) != h)(sent(i, g).wait_send)
@@ -546,8 +557,8 @@
             dma((Z,)),
             pltpu.SemaphoreType.REGULAR,
             pltpu.SemaphoreType.REGULAR,
-            dma((7,)),
-            dma((7,)),
+            dma((8,)),
+            dma((8,)),
             dma((HERE, halves)),
             dma((4, halves)),
         ],

time: 41.1 us -> 40.7 us (level)
  Pallas kernels: 40.9 us -> 40.3 us
    pallas_call x1, Pallas kernels: 38.6 us -> 37.9 us  [body(): pl.pallas_call(kernel, out_shape=jax.ShapeDtypeStruct((rows // HERE, HERE...]
where the time goes in v6:
time: 40.7 us; the launch traced here: 40.3 us
  Pallas kernels  40.3 us (99%)
    pallas_call x1, Pallas kernels, body(): pl.pallas_call(kernel, out_shape=jax.ShapeDtypeStruct((rows // HERE, HERE...  37.9 us
    pallas_call x1, Pallas kernels, body(): pl.pallas_call(settle, out_shape=jax.ShapeDtypeStruct(landed.shape, BF),...  2.4 us

profile of v6, /device:TPU:198, one launch (start us, length us, event | category | flops | bytes accessed | tf_op | source)
XLA Modules:
  0.0 40.3 jit_solution(6679948042639662315)
XLA Ops:
  0.0 37.9 %shard_map.55.src = bf16[256,4096]{1,0:T(8,128)(2,1)} custom-call(bf16[1024,1024]{1,0:T(8,128)(2,1)} %queries.1, bf16[1024,128]{1,0:T(8,128)(2,1)} %keys.1, bf16[1024,128]{1,0:T(8,128)(2,1)} %values.1, bf16[1,8]{1,0:T(2,128)(2,1)} %mid_pool.1, bf16[1,256]{1,0:T(2,128)(2,1)} %coarse_pool.1), custom_call_target="tpu_custom_call" | custom-call | tf_op jit(solution)/shard_map/pallas_call | solution.py:533
  37.9 2.4 %shard_map.56 = bf16[256,4096]{1,0:T(8,128)(2,1)} custom-call(bf16[256,4096]{1,0:T(8,128)(2,1)} %shard_map.55.src), custom_call_target="tpu_custom_call" | custom-call | tf_op jit(solution)/shard_map/pallas_call | solution.py:569
